TPU v7x, 512 devices: a whole 4x8x8 slice. The times are simulated.
512 devices in a mesh: resp: 128 (over z_hi, x, y), tp: 4 (over z_lo, core).
Axes of the slice: x: 4, y: 8, z: 8 (z_hi: 4, z_lo: 2; z = z_hi * 2 + z_lo), core: 2. Of those that a mesh axis runs over, the one named last changes fastest.
Arguments:
- response_queries: bfloat16 [256, 128, 4096], P('resp', None, 'tp'), may hold values from -1000 to 1000
- response_kv: bfloat16 [2, 256, 128, 2048], P(None, 'resp', None, 'tp'), may hold values from -6 to 6
- prompt_kv: bfloat16 [2, 16, 512, 2048], P(None, None, 'resp', 'tp'), may hold values from -16 to 16
- response_lengths: int32 [256], P('resp'), may hold values from 1 to 128, as said below
- device_prompt: int32 [128], replicated, may hold values from 0 to 15, as said below
- probe_weight: float32 [4096], P('tp'), may hold values from -0.5 to 0.5
Outputs:
- context: bfloat16 [256, 128, 4096], P('resp', None, 'tp')
- advantage: float32 [256], P('resp')
Inputs may be any that keep to these rules, and one draw needn't show every extreme that they name: `response_lengths`: at least one response has exactly 128 live tokens. `device_prompt`: each prompt index is named by exactly 8 entries.
All inputs are finite; a program needn't handle non-finite values.
Results may differ from a plain program's by a relative error of at most 0.0055.
Values may be sent and summed in bfloat16 or wider, within the bound.
A program may use at most 64 MiB of HBM per device.

v0:
```python
import math

import jax
import jax.numpy as jnp
from jax import lax
from jax.sharding import PartitionSpec as P

HEAD_DIM = 128
SCALAR = 144
BEST = 16


def attend_head(q_block, prefix_keys, prefix_values, self_keys, self_values, visible, score_scale):
    prompt_scores = (
        jnp.einsum("rtgd,pd->rtgp", q_block, prefix_keys, preferred_element_type=jnp.float32)
        * score_scale
    )
    self_scores = (
        jnp.einsum("rtgd,rud->rtgu", q_block, self_keys, preferred_element_type=jnp.float32)
        * score_scale
    )
    mask = visible[:, :, None, :]
    self_scores = jnp.where(mask, self_scores, -1e30)
    row_max = jnp.maximum(prompt_scores.max(-1), self_scores.max(-1))
    prompt_exp = jnp.exp(prompt_scores - row_max[..., None])
    self_exp = jnp.where(mask, jnp.exp(self_scores - row_max[..., None]), 0.0)
    denominator = prompt_exp.sum(-1) + self_exp.sum(-1)
    mixed = jnp.einsum(
        "rtgp,pd->rtgd",
        prompt_exp.astype(jnp.bfloat16),
        prefix_values,
        preferred_element_type=jnp.float32,
    )
    mixed = mixed + jnp.einsum(
        "rtgu,rud->rtgd",
        self_exp.astype(jnp.bfloat16),
        self_values,
        preferred_element_type=jnp.float32,
    )
    return mixed / denominator[..., None]


def shards(response_queries, response_kv, prompt_kv, response_lengths, device_prompt, probe_weight):
    rows = response_queries.shape[0]
    resp_len = response_queries.shape[1]
    kv_width = response_kv.shape[3]
    heads_local = response_queries.shape[2] // HEAD_DIM
    kv_local = kv_width // HEAD_DIM
    group_size = heads_local // kv_local
    score_scale = 1.0 / math.sqrt(SCALAR)
    my_index = lax.axis_index("resp")
    my_prompt = device_prompt[my_index]
    outgoing = jnp.take(prompt_kv, device_prompt, axis=1)
    arrived = lax.all_to_all(outgoing, "resp", split_axis=1, concat_axis=1, tiled=True)
    arrived = arrived.reshape(2, -1, kv_width)
    prefix_keys = arrived[0]
    prefix_values = arrived[1]
    positions = jnp.arange(resp_len, dtype=jnp.int32)
    causal = positions[None, :] <= positions[:, None]
    visible = causal[None, :, :] & (positions[None, None, :] < response_lengths[:, None, None])
    head_outputs = []
    for kv_head in range(kv_local):
        low = kv_head * HEAD_DIM
        q_block = response_queries[
            :, :, kv_head * group_size * HEAD_DIM : (kv_head + 1) * group_size * HEAD_DIM
        ]
        q_block = q_block.reshape(rows, resp_len, group_size, HEAD_DIM)
        mixed = attend_head(
            q_block,
            prefix_keys[:, low : low + HEAD_DIM],
            prefix_values[:, low : low + HEAD_DIM],
            response_kv[0, :, :, low : low + HEAD_DIM],
            response_kv[1, :, :, low : low + HEAD_DIM],
            visible,
            score_scale,
        )
        head_outputs.append(mixed.reshape(rows, resp_len, group_size * HEAD_DIM))
    joined = jnp.concatenate(head_outputs, axis=-1)
    live_rows = positions[None, :, None] < response_lengths[:, None, None]
    context = jnp.where(live_rows, joined, 0.0).astype(jnp.bfloat16)
    end_rows = jnp.take_along_axis(context, (response_lengths - 1)[:, None, None], axis=1)[:, 0]
    partial_value = jnp.sum(end_rows.astype(jnp.float32) * probe_weight, axis=-1)
    my_rewards = lax.psum(partial_value, "tp")
    table = lax.all_gather(my_rewards, "resp", axis=0, tiled=True)
    prompt_of = jnp.repeat(device_prompt, rows)
    same_prompt = (prompt_of == my_prompt).astype(jnp.float32)
    group_mean = jnp.sum(same_prompt * table) / BEST
    advantage = my_rewards - group_mean
    return (context, advantage)


def solution(mesh):
    placed = (
        P("resp", None, "tp"),
        P(None, "resp", None, "tp"),
        P(None, None, "resp", "tp"),
        P("resp"),
        P(),
        P("tp"),
    )
    return jax.shard_map(
        shards,
        mesh=mesh,
        in_specs=placed,
        out_specs=(P("resp", None, "tp"), P("resp")),
        check_vma=False,
    )
```

profile of v0, /device:TPU:64, one launch (start us, length us, event | category | flops | bytes accessed | tf_op | source)
XLA Modules:
  0.0 453.1 jit_solution(3612874274043894001)
XLA Ops:
  0.7 0.7 copy-done.24
  1.3 0.6 dynamic_slice.3
  1.9 0.7 broadcast_compare_fusion
  2.6 1.5 gather_fusion
  4.1 1.6 select_bitcast_fusion
  5.7 19.5 %all-to-all-start = ((bf16[2,128,4,512]{3,2,0,1:T(4,128)(2,1)}), bf16[2,128,4,512]{3,2,0,1:T(4,128)(2,1)S(1)}, u32[]{:S(2)}, u32[]{:S(2)}) async-start(bf16[2,128,4,512]{3,2,0,1:T(4,128)(2,1)} %select_bitcast_fusion), calls=%async_computation | async-start | bytes 2097152 | tf_op jit(solution)/shard_map/all_to_all | solution.py:54
  25.2 0.6 copy-done.25
  25.8 0.1 copy.58
  26.0 0.7 eq.12
  26.8 0.1 copy.98
  26.9 0.1 copy.95
  27.1 0.1 copy.92
  27.2 0.1 copy.101
  27.3 1.4 dynamic-slice
  28.7 0.8 or_reduce_fusion
  29.5 0.5 compare_and_fusion
  30.0 0.1 broadcast_and_fusion
  30.2 0.9 fusion.81
  31.0 0.9 fusion.83
  31.9 0.9 fusion.85
  32.8 0.9 fusion.87
  33.7 24.2 %all-to-all-done = bf16[2,128,4,512]{3,2,0,1:T(4,128)(2,1)S(1)} async-done(((bf16[2,128,4,512]{3,2,0,1:T(4,128)(2,1)}), bf16[2,128,4,512]{3,2,0,1:T(4,128)(2,1)S(1)}, u32[]{:S(2)}, u32[]{:S(2)}) %all-to-all-start) | async-done | bytes 1048608 | tf_op jit(solution)/shard_map/all_to_all | solution.py:54
  58.0 0.4 fusion.78
  58.4 0.1 squeeze.34
  58.5 0.8 copy-done.5
  59.2 0.9 fusion.80
  60.2 0.9 fusion.86
  61.0 0.9 squeeze.36
  62.0 0.7 copy-done.17
  62.6 0.2 fusion.19
  62.8 0.9 copy-done.1
  63.7 0.3 fusion.21
  64.0 0.7 copy-done.16
  64.7 0.2 fusion.17
  64.9 0.3 fusion.23
  65.2 0.3 fusion.84
  65.5 0.2 fusion.15
  65.7 0.3 fusion.25
  66.0 0.3 fusion.82
  66.3 0.3 fusion.27
  66.7 0.2 fusion.13
  66.9 0.4 copy-done.11
  67.3 0.2 copy-done.7
  67.4 0.2 copy-done.8
  67.8 0.2 fusion.33
  68.0 0.8 copy-done.15
  68.8 0.2 fusion.4
  69.1 0.1 copy.57
  69.2 0.2 fusion.6
  69.4 0.1 copy.56
  69.5 0.2 fusion.10
  69.8 0.1 copy.54
  69.9 0.2 fusion.8
  70.1 0.1 copy.55
  70.3 0.5 copy-done.21
  70.8 0.2 fusion.12
  70.9 0.5 copy-done.18
  71.5 0.6 gather_fusion.1
  72.1 0.2 multiply_reduce_fusion
  73.0 5.9 %psum.7 = f32[2]{0:T(128)S(1)} all-reduce(f32[2]{0:T(128)S(1)} %multiply_reduce_fusion), channel_id=1, replica_groups=mesh['resp'=128,'tp'=4] {'tp'}, use_global_device_ids=true, to_apply=%region_17.18 | all-reduce | flops 2 | bytes 16 | tf_op jit(solution)/shard_map/psum | solution.py:83
  78.9 0.2 dynamic-update-slice
  79.2 372.1 %all-reduce = f32[256]{0:T(256)S(1)} all-reduce(f32[256]{0:T(256)S(1)} %dynamic-update-slice), channel_id=1, replica_groups=mesh['resp'=128,'tp'=4] {'resp'}, use_global_device_ids=true, to_apply=%add | all-reduce | flops 256 | bytes 2048
  451.3 0.6 select_reduce_fusion
  452.5 0.5 broadcast_subtract_fusion
  (58 shorter events, 0.6 us)
Async XLA Ops:
  0.6 2.0 copy-start
  0.7 0.7 copy-start.24
  5.7 21.1 %copy-start.13 = (bf16[2,128,1024]{2,1,0:T(8,128)(2,1)S(1)}, bf16[2,128,1024]{2,1,0:T(8,128)(2,1)}, u32[]{:S(2)}) copy-start(bf16[2,128,1024]{2,1,0:T(8,128)(2,1)} %param.6) | copy-start | bytes 1572868
  5.7 52.3 %all-to-all-start = ((bf16[2,128,4,512]{3,2,0,1:T(4,128)(2,1)}), bf16[2,128,4,512]{3,2,0,1:T(4,128)(2,1)S(1)}, u32[]{:S(2)}, u32[]{:S(2)}) async-start(bf16[2,128,4,512]{3,2,0,1:T(4,128)(2,1)} %select_bitcast_fusion), calls=%async_computation | async-start | bytes 2097152 | tf_op jit(solution)/shard_map/all_to_all | solution.py:54
  25.2 0.7 copy-start.25
  26.8 3.4 copy-start.14
  26.9 5.9 %copy-start.2 = (bf16[2,128,256]{1,2,0:T(8,128)(2,1)}, bf16[2,128,256]{1,2,0:T(8,128)(2,1)S(1)}, u32[]{:S(2)}) copy-start(bf16[2,128,256]{1,2,0:T(8,128)(2,1)S(1)} %copy.98) | copy-start | bytes 393220
  27.3 3.7 copy-start.4
  29.5 0.6 copy-start.20
  30.1 2.7 copy-start.6
  58.3 0.9 copy-start.5
  59.2 0.9 copy-start.3
  62.0 0.7 copy-start.17
  62.6 1.0 copy-start.1
  64.0 0.7 copy-start.16
  66.3 1.0 copy-start.11
  66.7 0.8 copy-start.7
  66.7 1.0 copy-start.8
  66.7 1.0 copy-start.9
  66.7 1.1 copy-start.10
  67.8 1.0 copy-start.15
  70.1 0.7 copy-start.21
  70.8 0.7 copy-start.18
  71.4 381.6 %copy-start.12 = (bf16[2,128,1024]{2,1,0:T(8,128)(2,1)}, bf16[2,128,1024]{2,1,0:T(8,128)(2,1)S(1)}, u32[]{:S(2)}) copy-start(bf16[2,128,1024]{2,1,0:T(8,128)(2,1)S(1)} %fusion.12) | copy-start | bytes 1572868
  71.5 0.7 copy-start.19
  71.5 0.7 copy-start.23
  79.2 372.1 %copy-start.22 = (pred[256]{0:T(512)(128)(4,1)S(1)}, pred[256]{0:T(512)(128)(4,1)}, u32[]{:S(2)}) copy-start(pred[256]{0:T(512)(128)(4,1)} %eq.12) | copy-start | bytes 772
where the time goes:
time: 454 us; the launch traced here: 453 us
  blocking collectives  378 us (83%)
  waiting for transfers between devices  24.2 us (5%)
  starting transfers between devices  19.5 us (4%)
  local copies, waits for them, and re-layouts  14.8 us (3%)
  matrix products  8.07 us (2%)
  other arithmetic  6.03 us (1%)
    unnamed x1, blocking collectives  372 us
    all_to_all x1, waiting for transfers between devices, shards(): lax.all_to_all(outgoing, 'resp', split_axis=1, concat_axis=1, tiled=True)  24.2 us
    all_to_all x1, starting transfers between devices, shards(): lax.all_to_all(outgoing, 'resp', split_axis=1, concat_axis=1, tiled=True)  19.5 us
    unnamed x60, local copies, waits for them, and re-layouts  9.36 us
  transfers between devices with their start and end apart: 1, of which 1 were waited for; matrix products, arithmetic and copies ran while one was open for 2% of the time, Pallas kernels for 0%

commit v1 on v0

v1 whole, which is shorter than its diff:
```python
import functools
import math

import jax
import jax.numpy as jnp
from jax import lax
from jax.experimental import pallas as pl
from jax.experimental.pallas import tpu as pltpu
from jax.sharding import PartitionSpec as P

HEAD_DIM = 128
SCALAR = 144
BEST = 16
MESH = pl.DeviceIdType.MESH

NZ, NX, NY, NT = 4, 4, 8, 4
NXY, NZX, NZT = NX * NY, NZ * NX, NZ * NT
PROMPTS = 16
TOKENS = 4
PIECES = 4
ROWS = PIECES * TOKENS


def attention(scores_parts, values, scale2):
    top = functools.reduce(jnp.maximum, [jnp.max(s, axis=1, keepdims=True) for s in scores_parts])
    weights = [jnp.exp2((s - top) * scale2) for s in scores_parts]
    total = functools.reduce(jnp.add, [jnp.sum(w, axis=1, keepdims=True) for w in weights])
    mixed = functools.reduce(
        jnp.add,
        [
            jnp.dot(w.astype(jnp.bfloat16), v, preferred_element_type=jnp.float32)
            for w, v in zip(weights, values)
        ],
    )
    return mixed * (1.0 / total)


def scores_of(q, k):
    return lax.dot_general(q, k, (((1,), (1,)), ((), ())), preferred_element_type=jnp.float32)


def kernel(
    lengths,
    prompts,
    probe,
    q_hbm,
    kv_hbm,
    raw_hbm,
    context,
    advantage,
    q,
    kv,
    raw,
    own_a,
    own_b,
    got_a,
    got_b,
    out_a,
    out_b,
    all_a,
    all_b,
    row_1,
    row_2,
    load_sem,
    ring_send,
    ring_recv,
    send_sem,
    recv_sem,
):
    me = lax.axis_index("resp")
    tp = lax.axis_index("tp")
    zh = lax.div(me, NXY)
    xy = lax.rem(me, NXY)
    x = lax.div(xy, NY)
    y = lax.rem(xy, NY)
    zx = zh * NX + x

    def at_xy(j):
        return zh * NXY + j

    def at_zx(j):
        return j * NY + y

    def at_z(step):
        return lax.rem(zh + step, NZ) * NXY + xy

    def at_y(step):
        return zh * NXY + x * NY + lax.rem(y + step, NY)

    load_raw = pltpu.make_async_copy(raw_hbm, raw, load_sem.at[0])
    load_q = pltpu.make_async_copy(q_hbm, q, load_sem.at[1])
    load_kv = pltpu.make_async_copy(kv_hbm, kv, load_sem.at[2])
    load_raw.start()
    load_q.start()
    load_kv.start()

    barrier = pltpu.get_barrier_semaphore()

    def greet(device, tp_index):
        pl.semaphore_signal(barrier, inc=1, device_id=(device, tp_index), device_id_type=MESH)

    def greet_xy(i, c):
        greet(at_xy(lax.rem(xy + i, NXY)), tp)
        return c

    lax.fori_loop(1, NXY, greet_xy, 0)

    def greet_zx(i, c):
        greet(at_zx(lax.rem(zh + 1 + lax.div(i, NX), NZ) * NX + lax.rem(i, NX)), tp)
        return c

    lax.fori_loop(0, (NZ - 1) * NX, greet_zx, 0)

    def greet_tp(i, c):
        greet(lax.div(i, NT - 1) * NXY + xy, lax.rem(tp + 1 + lax.rem(i, NT - 1), NT))
        return c

    lax.fori_loop(0, NZ * (NT - 1), greet_tp, 0)

    load_raw.wait()

    def split(p, c):
        k = raw[0, p].astype(jnp.float32)
        v = raw[1, p].astype(jnp.float32)
        for plan, dst in enumerate((own_a, own_b)):
            parts = [
                part[:, (2 * plan + h) * HEAD_DIM : (2 * plan + h + 1) * HEAD_DIM]
                for part in (k, v)
                for h in range(2)
            ]
            dst[p] = jnp.concatenate(parts, axis=0).astype(jnp.bfloat16)
        return c

    lax.fori_loop(0, PROMPTS, split, 0)

    pl.semaphore_wait(barrier, (NXY - 1) + (NZ - 1) * NX + NZ * (NT - 1))

    half = PROMPTS // 2
    lo, hi = pl.ds(0, half), pl.ds(half, half)

    def ring(index, src, dst, device):
        return pltpu.make_async_remote_copy(
            src_ref=src,
            dst_ref=dst,
            send_sem=ring_send.at[index],
            recv_sem=ring_recv.at[index],
            device_id=(device, tp),
            device_id_type=MESH,
        )

    first = [
        ring(0, own_a, got_a.at[0], at_z(1)),
        ring(1, own_a, got_a.at[1], at_z(NZ - 1)),
        ring(2, own_b, got_b.at[2], at_y(2)),
        ring(3, own_b, got_b.at[3], at_y(NY - 2)),
        ring(4, own_b, got_b.at[0], at_y(1)),
        ring(5, own_b, got_b.at[1], at_y(NY - 1)),
    ]
    second = [
        ring(6, got_a.at[0, lo], got_a.at[2, lo], at_z(1)),
        ring(7, got_a.at[1, hi], got_a.at[2, hi], at_z(NZ - 1)),
        ring(8, got_b.at[2, lo], got_b.at[6, lo], at_y(2)),
        ring(9, got_b.at[2], got_b.at[4], at_y(1)),
        ring(10, got_b.at[3, hi], got_b.at[6, hi], at_y(NY - 2)),
        ring(11, got_b.at[3], got_b.at[5], at_y(NY - 1)),
    ]
    for copy in first:
        copy.start()
    first[0].wait_recv()
    second[0].start()
    first[1].wait_recv()
    second[1].start()
    first[2].wait_recv()
    second[2].start()
    second[3].start()
    first[3].wait_recv()
    second[4].start()
    second[5].start()
    second[0].wait_recv()
    second[1].wait_recv()

    def regroup(tiles):
        tiles = [t.astype(jnp.float32) for t in tiles]
        return [
            jnp.concatenate([t[TOKENS * g : TOKENS * (g + 1)] for t in tiles], axis=0).astype(jnp.bfloat16)
            for g in range(PIECES)
        ]

    def fill_a(dst, slot, p):
        for g, piece in enumerate(regroup([own_a[p]] + [got_a[s, p] for s in range(3)])):
            dst[slot, g] = piece

    def fill_b(dst, slot, p):
        for g, piece in enumerate(regroup([own_b[p]] + [got_b[s, p] for s in range(7)])):
            dst[slot, g] = piece

    def send_a(i, c):
        j = lax.rem(xy + i, NXY)
        fill_a(out_a, i, prompts[at_xy(j)])
        pltpu.make_async_remote_copy(
            src_ref=out_a.at[i],
            dst_ref=all_a.at[xy],
            send_sem=send_sem.at[0],
            recv_sem=recv_sem.at[0],
            device_id=(at_xy(j), tp),
            device_id_type=MESH,
        ).start()
        return c

    def send_b(i, c):
        j = lax.rem(zx + i, NZX)
        fill_b(out_b, i, prompts[at_zx(j)])
        pltpu.make_async_remote_copy(
            src_ref=out_b.at[i],
            dst_ref=all_b.at[zx],
            send_sem=send_sem.at[1],
            recv_sem=recv_sem.at[1],
            device_id=(at_zx(j), tp),
            device_id_type=MESH,
        ).start()
        return c

    lax.fori_loop(1, NXY // 2, send_a, 0)
    first[4].wait_recv()
    first[5].wait_recv()
    for copy in second[2:]:
        copy.wait_recv()

    def send_both(i, c):
        send_b(i, c)
        return send_a(i + NXY // 2 - 1, c)

    lax.fori_loop(1, NZX, send_both, 0)
    send_a(NXY - 1, 0)

    mine = prompts[me]
    fill_a(all_a, xy, mine)
    fill_b(all_b, zx, mine)

    load_q.wait()
    load_kv.wait()
    responses, steps, width = q.shape
    scale2 = math.log2(math.e) / math.sqrt(SCALAR)
    kv_heads = kv.shape[3] // HEAD_DIM
    column = lax.broadcasted_iota(jnp.int32, (8, steps), 1)
    last_q = []
    for r in range(responses):
        pick = (column == lengths[r] - 1).astype(jnp.bfloat16)
        last_q.append(jnp.dot(pick, q[r], preferred_element_type=jnp.float32).astype(jnp.bfloat16))

    def keys_values(g):
        ref = (all_a, all_b)[g // 2]
        h = g % 2
        return (
            ref[:, h].reshape(-1, HEAD_DIM),
            ref[:, 2 + h].reshape(-1, HEAD_DIM),
        )

    def own_keys_values(r, g):
        columns = slice(g * HEAD_DIM, (g + 1) * HEAD_DIM)
        return kv[0, r, :, columns], kv[1, r, :, columns]

    def wait_bytes(ref, sem):
        pltpu.make_async_copy(ref, ref, sem).wait()

    wait_bytes(all_a.at[pl.ds(0, NXY - 1)], recv_sem.at[0])
    wait_bytes(all_b.at[pl.ds(0, NZX - 1)], recv_sem.at[1])

    partial = [jnp.zeros((8, HEAD_DIM), jnp.float32) for _ in range(responses)]
    for g in range(kv_heads):
        k, v = keys_values(g)
        heads = (2 * g, 2 * g + 1)
        for r in range(responses):
            rows = jnp.concatenate(
                [last_q[r][:, h * HEAD_DIM : (h + 1) * HEAD_DIM] for h in heads], axis=0
            )
            own_k, own_v = own_keys_values(r, g)
            own = scores_of(rows, own_k)
            seen = lax.broadcasted_iota(jnp.int32, own.shape, 1) < lengths[r]
            own = jnp.where(seen, own, -1e30)
            mixed = attention([scores_of(rows, k), own], [v, own_v], scale2)
            mixed = mixed.astype(jnp.bfloat16).astype(jnp.float32)
            for n, h in enumerate(heads):
                partial[r] = partial[r] + mixed[8 * n : 8 * n + 8] * probe[h : h + 1, :]

    lane = lax.broadcasted_iota(jnp.int32, (1, HEAD_DIM), 1)
    sums = [jnp.sum(part[0:1], axis=1, keepdims=True) for part in partial]
    row = jnp.where(lane == mine, sums[0] + sums[1], 0.0)
    for r in range(responses):
        row = jnp.where(lane == PROMPTS + r, sums[r], row)

    zt = zh * NT + tp
    row_1[zt] = row

    def send_1(i, c):
        j = lax.rem(zt + i, NZT)
        pltpu.make_async_remote_copy(
            src_ref=row_1.at[zt],
            dst_ref=row_1.at[zt],
            send_sem=send_sem.at[2],
            recv_sem=recv_sem.at[2],
            device_id=(lax.div(j, NT) * NXY + xy, lax.rem(j, NT)),
            device_id_type=MESH,
        ).start()
        return c

    lax.fori_loop(1, NZT, send_1, 0)

    def attend(r, g):
        k, v = keys_values(g)
        own_k, own_v = own_keys_values(r, g)
        low = 2 * g * HEAD_DIM
        rows = jnp.concatenate(
            [q[r, :, low : low + HEAD_DIM], q[r, :, low + HEAD_DIM : low + 2 * HEAD_DIM]], axis=0
        )
        own = scores_of(rows, own_k)
        t = lax.broadcasted_iota(jnp.int32, own.shape, 0)
        t = jnp.where(t >= steps, t - steps, t)
        u = lax.broadcasted_iota(jnp.int32, own.shape, 1)
        own = jnp.where(u <= t, own, -1e30)
        mixed = attention([scores_of(rows, k), own], [v, own_v], scale2)
        live = lax.broadcasted_iota(jnp.int32, (steps, HEAD_DIM), 0) < lengths[r]
        for n in range(2):
            part = jnp.where(live, mixed[n * steps : (n + 1) * steps], 0.0)
            context[r, :, low + n * HEAD_DIM : low + (n + 1) * HEAD_DIM] = part.astype(jnp.bfloat16)

    for g in range(kv_heads // 2):
        for r in range(responses):
            attend(r, g)

    wait_bytes(row_1.at[pl.ds(0, NZT - 1)], recv_sem.at[2])
    line = jnp.sum(row_1[...], axis=0)
    rewards = jnp.sum(row_1[pl.ds(zh * NT, NT)], axis=0)
    row_2[xy] = line

    def send_2(i, c):
        j = lax.rem(xy + i, NXY)
        pltpu.make_async_remote_copy(
            src_ref=row_2.at[xy],
            dst_ref=row_2.at[xy],
            send_sem=send_sem.at[3],
            recv_sem=recv_sem.at[3],
            device_id=(at_xy(j), tp),
            device_id_type=MESH,
        ).start()
        return c

    lax.fori_loop(1, NXY, send_2, 0)

    for g in range(kv_heads // 2, kv_heads):
        for r in range(responses):
            attend(r, g)

    wait_bytes(row_2.at[pl.ds(0, NXY - 1)], recv_sem.at[3])
    table = jnp.sum(row_2[...], axis=0)
    group = jnp.sum(jnp.where(lane == mine, table, 0.0), axis=1, keepdims=True) / BEST
    result = rewards - group
    for r in range(responses):
        advantage[r] = jnp.sum(jnp.where(lane == PROMPTS + r, result, 0.0))

    for copy in first:
        copy.wait_send()
    for copy in second:
        copy.wait_send()
    wait_bytes(out_a.at[pl.ds(1, NXY - 1)], send_sem.at[0])
    wait_bytes(out_b.at[pl.ds(1, NZX - 1)], send_sem.at[1])
    wait_bytes(row_1.at[pl.ds(0, NZT - 1)], send_sem.at[2])
    wait_bytes(row_2.at[pl.ds(0, NXY - 1)], send_sem.at[3])


def shards(response_queries, response_kv, prompt_kv, response_lengths, device_prompt, probe_weight):
    bf16 = jnp.bfloat16
    smem = pl.BlockSpec(memory_space=pltpu.SMEM)
    vmem = pl.BlockSpec(memory_space=pltpu.VMEM)
    anywhere = pl.BlockSpec(memory_space=pl.ANY)
    block = (PROMPTS, ROWS, HEAD_DIM)
    context, advantage = pl.pallas_call(
        kernel,
        out_shape=(
            jax.ShapeDtypeStruct(response_queries.shape, bf16),
            jax.ShapeDtypeStruct(response_lengths.shape, jnp.float32),
        ),
        in_specs=[smem, smem, vmem, anywhere, anywhere, anywhere],
        out_specs=(vmem, smem),
        scratch_shapes=[
            pltpu.VMEM(response_queries.shape, bf16),
            pltpu.VMEM(response_kv.shape, bf16),
            pltpu.VMEM(prompt_kv.shape, bf16),
            pltpu.VMEM(block, bf16),
            pltpu.VMEM(block, bf16),
            pltpu.VMEM((NZ - 1,) + block, bf16),
            pltpu.VMEM((NY - 1,) + block, bf16),
            pltpu.VMEM((NXY, PIECES, NZ * TOKENS, HEAD_DIM), bf16),
            pltpu.VMEM((NZX, PIECES, NY * TOKENS, HEAD_DIM), bf16),
            pltpu.VMEM((NXY, PIECES, NZ * TOKENS, HEAD_DIM), bf16),
            pltpu.VMEM((NZX, PIECES, NY * TOKENS, HEAD_DIM), bf16),
            pltpu.VMEM((NZT, 1, HEAD_DIM), jnp.float32),
            pltpu.VMEM((NXY, 1, HEAD_DIM), jnp.float32),
            pltpu.SemaphoreType.DMA((3,)),
            pltpu.SemaphoreType.DMA((12,)),
            pltpu.SemaphoreType.DMA((12,)),
            pltpu.SemaphoreType.DMA((4,)),
            pltpu.SemaphoreType.DMA((4,)),
        ],
        compiler_params=pltpu.CompilerParams(
            collective_id=0, has_side_effects=True, vmem_limit_bytes=60 * 1024 * 1024
        ),
        cost_estimate=pl.CostEstimate(
            flops=700_000_000, bytes_accessed=2_000_000, transcendentals=1_400_000
        ),
    )(
        response_lengths,
        device_prompt,
        probe_weight.reshape(-1, HEAD_DIM),
        response_queries,
        response_kv,
        prompt_kv,
    )
    return context, advantage


def solution(mesh):
    placed = (
        P("resp", None, "tp"),
        P(None, "resp", None, "tp"),
        P(None, None, "resp", "tp"),
        P("resp"),
        P(),
        P("tp"),
    )
    return jax.shard_map(
        shards,
        mesh=mesh,
        in_specs=placed,
        out_specs=(P("resp", None, "tp"), P("resp")),
        check_vma=False,
    )
```

time: 454 us -> 59.2 us (0.13)
  the two profiles are of different devices: /device:TPU:64 before, /device:TPU:1 now
where the time goes in v1:
time: 59.2 us; the launch traced here: 59 us
  Pallas kernels  56 us (95%)
  local copies, waits for them, and re-layouts  2.38 us (4%)
  between operations  0.65 us (1%)
    pallas_call x1, Pallas kernels, shards(): pl.pallas_call(kernel, out_shape=(jax.ShapeDtypeStruct(response_queries.s...  56 us
    unnamed x4, local copies, waits for them, and re-layouts  2.38 us

profile of v1, /device:TPU:1, one launch (start us, length us, event | category | flops | bytes accessed | tf_op | source)
XLA Modules:
  0.0 59.0 jit_solution(2171376471541507512)
XLA Ops:
  0.6 56.0 %shard_map.77 = (bf16[2,128,1024]{2,1,0:T(8,128)(2,1)}, f32[2]{0:T(128)}) custom-call(s32[2]{0:T(128)} %lengths.1, s32[128]{0:T(128)} %prompts.1, f32[8,128]{1,0:T(8,128)} %bitcast.1, bf16[2,128,1024]{2,1,0:T(8,128)(2,1)} %q_hbm.1, bf16[2,2,128,512]{3,2,1,0:T(8,128)(2,1)} %kv_hbm.1, bf16[2,16,4,512]{3,2,1,0:T(4,128)(2,1)} %raw_hbm.1), custom_call_target="tpu_custom_call" | custom-call | flops 700000000 | bytes 2000000 | tf_op jit(solution)/shard_map/pallas_call | solution.py:377
  56.6 0.0 copy-start
  56.6 1.9 %copy.10 = bf16[2,128,1024]{2,1,0:T(8,128)(2,1)} copy(bf16[2,128,1024]{2,1,0:T(8,128)(2,1)} %get-tuple-element.4) | data formatting | bytes 1048576
  58.5 0.0 copy-done
  58.5 0.5 copy.11
Async XLA Ops:
  56.6 1.9 %copy-start = (f32[2]{0:T(128)S(1)}, f32[2]{0:T(128)}, u32[]{:S(2)}) copy-start(f32[2]{0:T(128)} %get-tuple-element.5) | copy-start | bytes 28

commit v2 on v1

--- a/solution.py
+++ b/solution.py
@@ -55,6 +55,8 @@
     own_b,
     got_a,
     got_b,
+    by_prompt_a,
+    by_prompt_b,
     out_a,
     out_b,
     all_a,
@@ -179,63 +181,73 @@
     second[0].wait_recv()
     second[1].wait_recv()
 
-    def regroup(tiles):
-        tiles = [t.astype(jnp.float32) for t in tiles]
-        return [
-            jnp.concatenate([t[TOKENS * g : TOKENS * (g + 1)] for t in tiles], axis=0).astype(jnp.bfloat16)
-            for g in range(PIECES)
-        ]
-
-    def fill_a(dst, slot, p):
-        for g, piece in enumerate(regroup([own_a[p]] + [got_a[s, p] for s in range(3)])):
-            dst[slot, g] = piece
-
-    def fill_b(dst, slot, p):
-        for g, piece in enumerate(regroup([own_b[p]] + [got_b[s, p] for s in range(7)])):
-            dst[slot, g] = piece
-
-    def send_a(i, c):
-        j = lax.rem(xy + i, NXY)
-        fill_a(out_a, i, prompts[at_xy(j)])
-        pltpu.make_async_remote_copy(
-            src_ref=out_a.at[i],
-            dst_ref=all_a.at[xy],
-            send_sem=send_sem.at[0],
-            recv_sem=recv_sem.at[0],
-            device_id=(at_xy(j), tp),
-            device_id_type=MESH,
-        ).start()
-        return c
-
-    def send_b(i, c):
-        j = lax.rem(zx + i, NZX)
-        fill_b(out_b, i, prompts[at_zx(j)])
-        pltpu.make_async_remote_copy(
-            src_ref=out_b.at[i],
-            dst_ref=all_b.at[zx],
-            send_sem=send_sem.at[1],
-            recv_sem=recv_sem.at[1],
-            device_id=(at_zx(j), tp),
-            device_id_type=MESH,
-        ).start()
-        return c
-
-    lax.fori_loop(1, NXY // 2, send_a, 0)
+    def regroup(own, got, slots, dst):
+        def one(p, c):
+            tiles = [own[p]] + [got[s, p] for s in range(slots)]
+            tiles = [t.astype(jnp.float32) for t in tiles]
+            for g in range(PIECES):
+                rows = [t[TOKENS * g : TOKENS * (g + 1)] for t in tiles]
+                dst[p, g] = jnp.concatenate(rows, axis=0).astype(jnp.bfloat16)
+            return c
+
+        def four(i, c):
+            for n in range(4):
+                one(4 * i + n, c)
+            return c
+
+        lax.fori_loop(0, PROMPTS // 4, four, 0)
+
+    def send(offsets_a, offsets_b):
+        places_a = [lax.rem(xy + i, NXY) for i in offsets_a]
+        places_b = [lax.rem(zx + i, NZX) for i in offsets_b]
+        blocks_b = [by_prompt_b[prompts[at_zx(j)]] for j in places_b]
+        blocks_a = [by_prompt_a[prompts[at_xy(j)]] for j in places_a]
+        for i, block in zip(offsets_b, blocks_b):
+            out_b[i] = block
+        for i, block in zip(offsets_a, blocks_a):
+            out_a[i] = block
+        for i, j in zip(offsets_b, places_b):
+            pltpu.make_async_remote_copy(
+                src_ref=out_b.at[i],
+                dst_ref=all_b.at[zx],
+                send_sem=send_sem.at[1],
+                recv_sem=recv_sem.at[1],
+                device_id=(at_zx(j), tp),
+                device_id_type=MESH,
+            ).start()
+        for i, j in zip(offsets_a, places_a):
+            pltpu.make_async_remote_copy(
+                src_ref=out_a.at[i],
+                dst_ref=all_a.at[xy],
+                send_sem=send_sem.at[0],
+                recv_sem=recv_sem.at[0],
+                device_id=(at_xy(j), tp),
+                device_id_type=MESH,
+            ).start()
+
+    regroup(own_a, got_a, NZ - 1, by_prompt_a)
+
+    def send_all_a(i, c):
+        send([6 * i + 1 + n for n in range(6)], [])
+        return c
+
+    lax.fori_loop(0, 5, send_all_a, 0)
+    send([NXY - 1], [])
     first[4].wait_recv()
     first[5].wait_recv()
     for copy in second[2:]:
         copy.wait_recv()
-
-    def send_both(i, c):
-        send_b(i, c)
-        return send_a(i + NXY // 2 - 1, c)
-
-    lax.fori_loop(1, NZX, send_both, 0)
-    send_a(NXY - 1, 0)
+    regroup(own_b, got_b, NY - 1, by_prompt_b)
+
+    def send_all_b(i, c):
+        send([], [5 * i + 1 + n for n in range(5)])
+        return c
+
+    lax.fori_loop(0, 3, send_all_b, 0)
 
     mine = prompts[me]
-    fill_a(all_a, xy, mine)
-    fill_b(all_b, zx, mine)
+    all_a[xy] = by_prompt_a[mine]
+    all_b[zx] = by_prompt_b[mine]
 
     load_q.wait()
     load_kv.wait()
@@ -263,11 +275,9 @@
     def wait_bytes(ref, sem):
         pltpu.make_async_copy(ref, ref, sem).wait()
 
-    wait_bytes(all_a.at[pl.ds(0, NXY - 1)], recv_sem.at[0])
-    wait_bytes(all_b.at[pl.ds(0, NZX - 1)], recv_sem.at[1])
-
     partial = [jnp.zeros((8, HEAD_DIM), jnp.float32) for _ in range(responses)]
-    for g in range(kv_heads):
+
+    def reward_of(g):
         k, v = keys_values(g)
         heads = (2 * g, 2 * g + 1)
         for r in range(responses):
@@ -282,29 +292,6 @@
             mixed = mixed.astype(jnp.bfloat16).astype(jnp.float32)
             for n, h in enumerate(heads):
                 partial[r] = partial[r] + mixed[8 * n : 8 * n + 8] * probe[h : h + 1, :]
-
-    lane = lax.broadcasted_iota(jnp.int32, (1, HEAD_DIM), 1)
-    sums = [jnp.sum(part[0:1], axis=1, keepdims=True) for part in partial]
-    row = jnp.where(lane == mine, sums[0] + sums[1], 0.0)
-    for r in range(responses):
-        row = jnp.where(lane == PROMPTS + r, sums[r], row)
-
-    zt = zh * NT + tp
-    row_1[zt] = row
-
-    def send_1(i, c):
-        j = lax.rem(zt + i, NZT)
-        pltpu.make_async_remote_copy(
-            src_ref=row_1.at[zt],
-            dst_ref=row_1.at[zt],
-            send_sem=send_sem.at[2],
-            recv_sem=recv_sem.at[2],
-            device_id=(lax.div(j, NT) * NXY + xy, lax.rem(j, NT)),
-            device_id_type=MESH,
-        ).start()
-        return c
-
-    lax.fori_loop(1, NZT, send_1, 0)
 
     def attend(r, g):
         k, v = keys_values(g)
@@ -324,16 +311,46 @@
             part = jnp.where(live, mixed[n * steps : (n + 1) * steps], 0.0)
             context[r, :, low + n * HEAD_DIM : low + (n + 1) * HEAD_DIM] = part.astype(jnp.bfloat16)
 
-    for g in range(kv_heads // 2):
+    wait_bytes(all_a.at[pl.ds(0, NXY - 1)], recv_sem.at[0])
+    for g in range(2):
+        reward_of(g)
+    for g in range(2):
         for r in range(responses):
             attend(r, g)
+
+    wait_bytes(all_b.at[pl.ds(0, NZX - 1)], recv_sem.at[1])
+    for g in range(2, kv_heads):
+        reward_of(g)
+
+    lane = lax.broadcasted_iota(jnp.int32, (1, HEAD_DIM), 1)
+    sums = [jnp.sum(part[0:1], axis=1, keepdims=True) for part in partial]
+    row = jnp.where(lane == mine, sums[0] + sums[1], 0.0)
+    for r in range(responses):
+        row = jnp.where(lane == PROMPTS + r, sums[r], row)
+
+    zt = zh * NT + tp
+    row_1[zt] = row
+
+    for i in range(1, NZT):
+        j = lax.rem(zt + i, NZT)
+        pltpu.make_async_remote_copy(
+            src_ref=row_1.at[zt],
+            dst_ref=row_1.at[zt],
+            send_sem=send_sem.at[2],
+            recv_sem=recv_sem.at[2],
+            device_id=(lax.div(j, NT) * NXY + xy, lax.rem(j, NT)),
+            device_id_type=MESH,
+        ).start()
+
+    for r in range(responses):
+        attend(r, 2)
 
     wait_bytes(row_1.at[pl.ds(0, NZT - 1)], recv_sem.at[2])
     line = jnp.sum(row_1[...], axis=0)
     rewards = jnp.sum(row_1[pl.ds(zh * NT, NT)], axis=0)
     row_2[xy] = line
 
-    def send_2(i, c):
+    for i in range(1, NXY):
         j = lax.rem(xy + i, NXY)
         pltpu.make_async_remote_copy(
             src_ref=row_2.at[xy],
@@ -343,13 +360,9 @@
             device_id=(at_xy(j), tp),
             device_id_type=MESH,
         ).start()
-        return c
-
-    lax.fori_loop(1, NXY, send_2, 0)
-
-    for g in range(kv_heads // 2, kv_heads):
-        for r in range(responses):
-            attend(r, g)
+
+    for r in range(responses):
+        attend(r, 3)
 
     wait_bytes(row_2.at[pl.ds(0, NXY - 1)], recv_sem.at[3])
     table = jnp.sum(row_2[...], axis=0)
@@ -373,11 +386,12 @@
     smem = pl.BlockSpec(memory_space=pltpu.SMEM)
     vmem = pl.BlockSpec(memory_space=pltpu.VMEM)
     anywhere = pl.BlockSpec(memory_space=pl.ANY)
+    in_hbm = functools.partial(pltpu.with_memory_space_constraint, memory_space=pltpu.HBM)
     block = (PROMPTS, ROWS, HEAD_DIM)
     context, advantage = pl.pallas_call(
         kernel,
         out_shape=(
-            jax.ShapeDtypeStruct(response_queries.shape, bf16),
+            pltpu.VMEM(response_queries.shape, bf16),
             jax.ShapeDtypeStruct(response_lengths.shape, jnp.float32),
         ),
         in_specs=[smem, smem, vmem, anywhere, anywhere, anywhere],
@@ -390,6 +404,8 @@
             pltpu.VMEM(block, bf16),
             pltpu.VMEM((NZ - 1,) + block, bf16),
             pltpu.VMEM((NY - 1,) + block, bf16),
+            pltpu.VMEM((PROMPTS, PIECES, NZ * TOKENS, HEAD_DIM), bf16),
+            pltpu.VMEM((PROMPTS, PIECES, NY * TOKENS, HEAD_DIM), bf16),
             pltpu.VMEM((NXY, PIECES, NZ * TOKENS, HEAD_DIM), bf16),
             pltpu.VMEM((NZX, PIECES, NY * TOKENS, HEAD_DIM), bf16),
             pltpu.VMEM((NXY, PIECES, NZ * TOKENS, HEAD_DIM), bf16),
@@ -403,18 +419,18 @@
             pltpu.SemaphoreType.DMA((4,)),
         ],
         compiler_params=pltpu.CompilerParams(
-            collective_id=0, has_side_effects=True, vmem_limit_bytes=60 * 1024 * 1024
+            collective_id=0, has_side_effects=True, vmem_limit_bytes=48 * 1024 * 1024
         ),
         cost_estimate=pl.CostEstimate(
             flops=700_000_000, bytes_accessed=2_000_000, transcendentals=1_400_000
         ),
     )(
-        response_lengths,
-        device_prompt,
-        probe_weight.reshape(-1, HEAD_DIM),
-        response_queries,
-        response_kv,
-        prompt_kv,
+        in_hbm(response_lengths),
+        in_hbm(device_prompt),
+        in_hbm(probe_weight.reshape(-1, HEAD_DIM)),
+        in_hbm(response_queries),
+        in_hbm(response_kv),
+        in_hbm(prompt_kv),
     )
     return context, advantage
 

time: 59.2 us -> 57.9 us (0.978)
  local copies, waits for them, and re-layouts: 2.38 us -> 1.31 us
    unnamed x4 -> x2, local copies, waits for them, and re-layouts: 2.38 us -> 1.31 us
where the time goes in v2:
time: 57.9 us; the launch traced here: 57.8 us
  Pallas kernels  55.8 us (96%)
  local copies, waits for them, and re-layouts  1.31 us (2%)
  between operations  0.64 us (1%)
    pallas_call x1, Pallas kernels, shards(): pl.pallas_call(kernel, out_shape=(pltpu.VMEM(response_queries.shape, bf16...  55.8 us
    unnamed x2, local copies, waits for them, and re-layouts  1.31 us

profile of v2, /device:TPU:1, one launch (start us, length us, event | category | flops | bytes accessed | tf_op | source)
XLA Modules:
  0.0 57.8 jit_solution(322875748326113283)
XLA Ops:
  0.6 55.8 %shard_map.77 = (bf16[2,128,1024]{2,1,0:T(8,128)(2,1)S(1)}, f32[2]{0:T(128)S(1)}) custom-call(s32[2]{0:T(128)} %lengths.1, s32[128]{0:T(128)} %prompts.1, f32[8,128]{1,0:T(8,128)} %bitcast.1, bf16[2,128,1024]{2,1,0:T(8,128)(2,1)} %q_hbm.1, bf16[2,2,128,512]{3,2,1,0:T(8,128)(2,1)} %kv_hbm.1, bf16[2,16,4,512]{3,2,1,0:T(4,128)(2,1)} %raw_hbm.1), custom_call_target="tpu_custom_call" | custom-call | flops 700000000 | bytes 2000000 | tf_op jit(solution)/shard_map/pallas_call | solution.py:391
  56.5 0.8 %copy.10 = bf16[2,128,1024]{2,1,0:T(8,128)(2,1)} copy(bf16[2,128,1024]{2,1,0:T(8,128)(2,1)S(1)} %get-tuple-element.2) | data formatting | bytes 1048576
  57.3 0.5 copy.11

commit v3 on v2

v3 whole, which is shorter than its diff:
```python
import functools
import math

import jax
import jax.numpy as jnp
from jax import lax
from jax.experimental import pallas as pl
from jax.experimental.pallas import tpu as pltpu
from jax.sharding import PartitionSpec as P

HEAD_DIM = 128
SCALAR = 144
BEST = 16
MESH = pl.DeviceIdType.MESH

NZ, NX, NY, NT = 4, 4, 8, 4
NXY, NZX, NZT = NX * NY, NZ * NX, NZ * NT
PROMPTS = 16
TOKENS = 4
PIECES = 4
ROWS = PIECES * TOKENS


def attention(scores_parts, values, scale2):
    top = functools.reduce(jnp.maximum, [jnp.max(s, axis=1, keepdims=True) for s in scores_parts])
    weights = [jnp.exp2((s - top) * scale2) for s in scores_parts]
    total = functools.reduce(jnp.add, [jnp.sum(w, axis=1, keepdims=True) for w in weights])
    mixed = functools.reduce(
        jnp.add,
        [
            jnp.dot(w.astype(jnp.bfloat16), v, preferred_element_type=jnp.float32)
            for w, v in zip(weights, values)
        ],
    )
    return mixed * (1.0 / total)


def wait_bytes(ref, sem):
    pltpu.make_async_copy(ref, ref, sem).wait()


def scores_of(q, k):
    return lax.dot_general(q, k, (((1,), (1,)), ((), ())), preferred_element_type=jnp.float32)


def gather_kernel(
    prompts,
    raw_hbm,
    all_a,
    all_b,
    raw,
    own_a,
    own_b,
    got_a,
    got_b,
    by_prompt_a,
    by_prompt_b,
    out_a,
    out_b,
    load_sem,
    ring_send,
    ring_recv,
    send_sem,
    recv_sem,
):
    me = lax.axis_index("resp")
    tp = lax.axis_index("tp")
    zh = lax.div(me, NXY)
    xy = lax.rem(me, NXY)
    x = lax.div(xy, NY)
    y = lax.rem(xy, NY)
    zx = zh * NX + x

    def at_xy(j):
        return zh * NXY + j

    def at_zx(j):
        return j * NY + y

    def at_z(step):
        return lax.rem(zh + step, NZ) * NXY + xy

    def at_y(step):
        return zh * NXY + x * NY + lax.rem(y + step, NY)

    load_raw = pltpu.make_async_copy(raw_hbm, raw, load_sem.at[0])
    load_raw.start()

    barrier = pltpu.get_barrier_semaphore()

    def greet(device, tp_index):
        pl.semaphore_signal(barrier, inc=1, device_id=(device, tp_index), device_id_type=MESH)

    def greet_xy(i, c):
        greet(at_xy(lax.rem(xy + i, NXY)), tp)
        return c

    lax.fori_loop(1, NXY, greet_xy, 0)

    def greet_zx(i, c):
        greet(at_zx(lax.rem(zh + 1 + lax.div(i, NX), NZ) * NX + lax.rem(i, NX)), tp)
        return c

    lax.fori_loop(0, (NZ - 1) * NX, greet_zx, 0)

    load_raw.wait()

    def split(p, c):
        k = raw[0, p].astype(jnp.float32)
        v = raw[1, p].astype(jnp.float32)
        for plan, dst in enumerate((own_a, own_b)):
            parts = [
                part[:, (2 * plan + h) * HEAD_DIM : (2 * plan + h + 1) * HEAD_DIM]
                for part in (k, v)
                for h in range(2)
            ]
            dst[p] = jnp.concatenate(parts, axis=0).astype(jnp.bfloat16)
        return c

    lax.fori_loop(0, PROMPTS, split, 0)

    pl.semaphore_wait(barrier, (NXY - 1) + (NZ - 1) * NX)

    half = PROMPTS // 2
    lo, hi = pl.ds(0, half), pl.ds(half, half)

    def ring(index, src, dst, device):
        return pltpu.make_async_remote_copy(
            src_ref=src,
            dst_ref=dst,
            send_sem=ring_send.at[index],
            recv_sem=ring_recv.at[index],
            device_id=(device, tp),
            device_id_type=MESH,
        )

    first = [
        ring(0, own_a, got_a.at[0], at_z(1)),
        ring(1, own_a, got_a.at[1], at_z(NZ - 1)),
        ring(2, own_b, got_b.at[2], at_y(2)),
        ring(3, own_b, got_b.at[3], at_y(NY - 2)),
        ring(4, own_b, got_b.at[0], at_y(1)),
        ring(5, own_b, got_b.at[1], at_y(NY - 1)),
    ]
    second = [
        ring(6, got_a.at[0, lo], got_a.at[2, lo], at_z(1)),
        ring(7, got_a.at[1, hi], got_a.at[2, hi], at_z(NZ - 1)),
        ring(8, got_b.at[2, lo], got_b.at[6, lo], at_y(2)),
        ring(9, got_b.at[2], got_b.at[4], at_y(1)),
        ring(10, got_b.at[3, hi], got_b.at[6, hi], at_y(NY - 2)),
        ring(11, got_b.at[3], got_b.at[5], at_y(NY - 1)),
    ]
    for copy in first:
        copy.start()
    first[0].wait_recv()
    second[0].start()
    first[1].wait_recv()
    second[1].start()
    first[2].wait_recv()
    second[2].start()
    second[3].start()
    first[3].wait_recv()
    second[4].start()
    second[5].start()
    second[0].wait_recv()
    second[1].wait_recv()

    def regroup(own, got, slots, dst):
        def one(p, c):
            tiles = [own[p]] + [got[s, p] for s in range(slots)]
            tiles = [t.astype(jnp.float32) for t in tiles]
            for g in range(PIECES):
                rows = [t[TOKENS * g : TOKENS * (g + 1)] for t in tiles]
                dst[p, g] = jnp.concatenate(rows, axis=0).astype(jnp.bfloat16)
            return c

        def four(i, c):
            for n in range(4):
                one(4 * i + n, c)
            return c

        lax.fori_loop(0, PROMPTS // 4, four, 0)

    def send(offsets_a, offsets_b):
        places_a = [lax.rem(xy + i, NXY) for i in offsets_a]
        places_b = [lax.rem(zx + i, NZX) for i in offsets_b]
        blocks_b = [by_prompt_b[prompts[at_zx(j)]] for j in places_b]
        blocks_a = [by_prompt_a[prompts[at_xy(j)]] for j in places_a]
        for i, block in zip(offsets_b, blocks_b):
            out_b[i] = block
        for i, block in zip(offsets_a, blocks_a):
            out_a[i] = block
        for i, j in zip(offsets_b, places_b):
            pltpu.make_async_remote_copy(
                src_ref=out_b.at[i],
                dst_ref=all_b.at[zx],
                send_sem=send_sem.at[1],
                recv_sem=recv_sem.at[1],
                device_id=(at_zx(j), tp),
                device_id_type=MESH,
            ).start()
        for i, j in zip(offsets_a, places_a):
            pltpu.make_async_remote_copy(
                src_ref=out_a.at[i],
                dst_ref=all_a.at[xy],
                send_sem=send_sem.at[0],
                recv_sem=recv_sem.at[0],
                device_id=(at_xy(j), tp),
                device_id_type=MESH,
            ).start()

    regroup(own_a, got_a, NZ - 1, by_prompt_a)

    def send_all_a(i, c):
        send([6 * i + 1 + n for n in range(6)], [])
        return c

    lax.fori_loop(0, 5, send_all_a, 0)
    send([NXY - 1], [])
    first[4].wait_recv()
    first[5].wait_recv()
    for copy in second[2:]:
        copy.wait_recv()
    regroup(own_b, got_b, NY - 1, by_prompt_b)

    def send_all_b(i, c):
        send([], [5 * i + 1 + n for n in range(5)])
        return c

    lax.fori_loop(0, 3, send_all_b, 0)

    mine = prompts[me]
    all_a[xy] = by_prompt_a[mine]
    all_b[zx] = by_prompt_b[mine]

    wait_bytes(all_a.at[pl.ds(0, NXY - 1)], recv_sem.at[0])
    wait_bytes(all_b.at[pl.ds(0, NZX - 1)], recv_sem.at[1])
    for copy in first:
        copy.wait_send()
    for copy in second:
        copy.wait_send()
    wait_bytes(out_a.at[pl.ds(1, NXY - 1)], send_sem.at[0])
    wait_bytes(out_b.at[pl.ds(1, NZX - 1)], send_sem.at[1])


def attention_kernel(lengths, probe, q, kv, all_a, all_b, context, reward):
    responses, steps, width = q.shape
    scale2 = math.log2(math.e) / math.sqrt(SCALAR)
    kv_heads = kv.shape[3] // HEAD_DIM
    place = lax.broadcasted_iota(jnp.int32, (steps, HEAD_DIM), 0)
    sums = [jnp.zeros((1, HEAD_DIM), jnp.float32) for _ in range(responses)]
    for g in range(kv_heads):
        blocks, h = (all_a, all_b)[g // 2], g % 2
        k = blocks[:, h].reshape(-1, HEAD_DIM)
        v = blocks[:, 2 + h].reshape(-1, HEAD_DIM)
        columns = slice(g * HEAD_DIM, (g + 1) * HEAD_DIM)
        for r in range(responses):
            low = 2 * g * HEAD_DIM
            rows = jnp.concatenate(
                [q[r, :, low : low + HEAD_DIM], q[r, :, low + HEAD_DIM : low + 2 * HEAD_DIM]], axis=0
            )
            own = scores_of(rows, kv[0, r, :, columns])
            t = lax.broadcasted_iota(jnp.int32, own.shape, 0)
            t = jnp.where(t >= steps, t - steps, t)
            u = lax.broadcasted_iota(jnp.int32, own.shape, 1)
            own = jnp.where(u <= t, own, -1e30)
            mixed = attention([scores_of(rows, k), own], [v, kv[1, r, :, columns]], scale2)
            for n in range(2):
                part = mixed[n * steps : (n + 1) * steps]
                part = jnp.where(place < lengths[r], part, 0.0).astype(jnp.bfloat16)
                context[r, :, low + n * HEAD_DIM : low + (n + 1) * HEAD_DIM] = part
                last = jnp.where(place == lengths[r] - 1, part.astype(jnp.float32), 0.0)
                last = jnp.sum(last, axis=0, keepdims=True)
                sums[r] = sums[r] + last * probe[2 * g + n : 2 * g + n + 1, :]
    for r in range(responses):
        reward[r] = sums[r]


def reward_kernel(prompts, reward, advantage, row_1, row_2, send_sem, recv_sem):
    responses = reward.shape[0]
    me = lax.axis_index("resp")
    tp = lax.axis_index("tp")
    zh = lax.div(me, NXY)
    xy = lax.rem(me, NXY)
    zt = zh * NT + tp
    mine = prompts[me]

    def at_xy(j):
        return zh * NXY + j

    def at_zt(j):
        return (lax.div(j, NT) * NXY + xy, lax.rem(j, NT))

    barrier = pltpu.get_barrier_semaphore()
    for i in range(1, NZT):
        device = at_zt(lax.rem(zt + i, NZT))
        pl.semaphore_signal(barrier, inc=1, device_id=device, device_id_type=MESH)
    for i in range(1, NXY):
        device = (at_xy(lax.rem(xy + i, NXY)), tp)
        pl.semaphore_signal(barrier, inc=1, device_id=device, device_id_type=MESH)

    lane = lax.broadcasted_iota(jnp.int32, (1, HEAD_DIM), 1)
    sums = [jnp.sum(reward[r], axis=1, keepdims=True) for r in range(responses)]
    row = jnp.where(lane == mine, sums[0] + sums[1], 0.0)
    for r in range(responses):
        row = jnp.where(lane == PROMPTS + r, sums[r], row)

    row_1[zt] = row
    pl.semaphore_wait(barrier, (NZT - 1) + (NXY - 1))

    for i in range(1, NZT):
        pltpu.make_async_remote_copy(
            src_ref=row_1.at[zt],
            dst_ref=row_1.at[zt],
            send_sem=send_sem.at[0],
            recv_sem=recv_sem.at[0],
            device_id=at_zt(lax.rem(zt + i, NZT)),
            device_id_type=MESH,
        ).start()

    wait_bytes(row_1.at[pl.ds(0, NZT - 1)], recv_sem.at[0])
    line = jnp.sum(row_1[...], axis=0)
    rewards = jnp.sum(row_1[pl.ds(zh * NT, NT)], axis=0)
    row_2[xy] = line

    for i in range(1, NXY):
        j = lax.rem(xy + i, NXY)
        pltpu.make_async_remote_copy(
            src_ref=row_2.at[xy],
            dst_ref=row_2.at[xy],
            send_sem=send_sem.at[1],
            recv_sem=recv_sem.at[1],
            device_id=(at_xy(j), tp),
            device_id_type=MESH,
        ).start()

    wait_bytes(row_2.at[pl.ds(0, NXY - 1)], recv_sem.at[1])
    table = jnp.sum(row_2[...], axis=0)
    group = jnp.sum(jnp.where(lane == mine, table, 0.0), axis=1, keepdims=True) / BEST
    result = rewards - group
    for r in range(responses):
        advantage[r] = jnp.sum(jnp.where(lane == PROMPTS + r, result, 0.0))

    wait_bytes(row_1.at[pl.ds(0, NZT - 1)], send_sem.at[0])
    wait_bytes(row_2.at[pl.ds(0, NXY - 1)], send_sem.at[1])


def shards(response_queries, response_kv, prompt_kv, response_lengths, device_prompt, probe_weight):
    bf16 = jnp.bfloat16
    smem = pl.BlockSpec(memory_space=pltpu.SMEM)
    vmem = pl.BlockSpec(memory_space=pltpu.VMEM)
    anywhere = pl.BlockSpec(memory_space=pl.ANY)
    in_hbm = functools.partial(pltpu.with_memory_space_constraint, memory_space=pltpu.HBM)
    in_vmem = functools.partial(pltpu.with_memory_space_constraint, memory_space=pltpu.VMEM)
    block = (PROMPTS, ROWS, HEAD_DIM)
    blocks_a = (NXY, PIECES, NZ * TOKENS, HEAD_DIM)
    blocks_b = (NZX, PIECES, NY * TOKENS, HEAD_DIM)
    all_a, all_b = pl.pallas_call(
        gather_kernel,
        out_shape=(pltpu.VMEM(blocks_a, bf16), pltpu.VMEM(blocks_b, bf16)),
        in_specs=[smem, anywhere],
        out_specs=(vmem, vmem),
        scratch_shapes=[
            pltpu.VMEM(prompt_kv.shape, bf16),
            pltpu.VMEM(block, bf16),
            pltpu.VMEM(block, bf16),
            pltpu.VMEM((NZ - 1,) + block, bf16),
            pltpu.VMEM((NY - 1,) + block, bf16),
            pltpu.VMEM((PROMPTS,) + blocks_a[1:], bf16),
            pltpu.VMEM((PROMPTS,) + blocks_b[1:], bf16),
            pltpu.VMEM(blocks_a, bf16),
            pltpu.VMEM(blocks_b, bf16),
            pltpu.SemaphoreType.DMA((1,)),
            pltpu.SemaphoreType.DMA((12,)),
            pltpu.SemaphoreType.DMA((12,)),
            pltpu.SemaphoreType.DMA((2,)),
            pltpu.SemaphoreType.DMA((2,)),
        ],
        compiler_params=pltpu.CompilerParams(
            collective_id=0, has_side_effects=True, vmem_limit_bytes=32 * 1024 * 1024
        ),
        cost_estimate=pl.CostEstimate(flops=1_000_000, bytes_accessed=2_000_000, transcendentals=0),
    )(in_hbm(device_prompt), in_hbm(prompt_kv))
    context, reward = pl.pallas_call(
        attention_kernel,
        out_shape=(
            jax.ShapeDtypeStruct(response_queries.shape, bf16),
            jax.ShapeDtypeStruct((response_lengths.shape[0], 1, HEAD_DIM), jnp.float32),
        ),
        in_specs=[smem, vmem, vmem, vmem, vmem, vmem],
        out_specs=(vmem, vmem),
        compiler_params=pltpu.CompilerParams(vmem_limit_bytes=32 * 1024 * 1024),
        cost_estimate=pl.CostEstimate(
            flops=700_000_000, bytes_accessed=2_000_000, transcendentals=1_400_000
        ),
    )(
        response_lengths,
        probe_weight.reshape(-1, HEAD_DIM),
        response_queries,
        response_kv,
        in_vmem(all_a),
        in_vmem(all_b),
    )
    advantage = pl.pallas_call(
        reward_kernel,
        out_shape=jax.ShapeDtypeStruct(response_lengths.shape, jnp.float32),
        in_specs=[smem, vmem],
        out_specs=smem,
        scratch_shapes=[
            pltpu.VMEM((NZT, 1, HEAD_DIM), jnp.float32),
            pltpu.VMEM((NXY, 1, HEAD_DIM), jnp.float32),
            pltpu.SemaphoreType.DMA((2,)),
            pltpu.SemaphoreType.DMA((2,)),
        ],
        compiler_params=pltpu.CompilerParams(collective_id=1, has_side_effects=True),
        cost_estimate=pl.CostEstimate(flops=10_000, bytes_accessed=10_000, transcendentals=0),
    )(device_prompt, reward)
    return context, advantage


def solution(mesh):
    placed = (
        P("resp", None, "tp"),
        P(None, "resp", None, "tp"),
        P(None, None, "resp", "tp"),
        P("resp"),
        P(),
        P("tp"),
    )
    return jax.shard_map(
        shards,
        mesh=mesh,
        in_specs=placed,
        out_specs=(P("resp", None, "tp"), P("resp")),
        check_vma=False,
    )
```

time: 57.9 us -> 68.9 us (1.19)
  Pallas kernels: 55.8 us -> 63.5 us
  local copies, waits for them, and re-layouts: 1.31 us -> 4.42 us
    pallas_call x1 -> x3, Pallas kernels: 55.8 us -> 63.5 us  [the longest x1 37.9 us: shards(): pl.pallas_call(gather_kernel, out_shape=(pltpu.VMEM(blocks_a, bf16), pltp...]
    unnamed x2 -> x11, local copies, waits for them, and re-layouts: 1.31 us -> 4.42 us
where the time goes in v3:
time: 68.9 us; the launch traced here: 68.6 us
  Pallas kernels  63.5 us (92%)
  local copies, waits for them, and re-layouts  4.42 us (6%)
    pallas_call x1, Pallas kernels, shards(): pl.pallas_call(gather_kernel, out_shape=(pltpu.VMEM(blocks_a, bf16), pltp...  37.9 us
    pallas_call x1, Pallas kernels, shards(): pl.pallas_call(reward_kernel, out_shape=jax.ShapeDtypeStruct(response_len...  21 us
    pallas_call x1, Pallas kernels, shards(): pl.pallas_call(attention_kernel, out_shape=(jax.ShapeDtypeStruct(response...  4.52 us
    unnamed x11, local copies, waits for them, and re-layouts  4.42 us

profile of v3, /device:TPU:1, one launch (start us, length us, event | category | flops | bytes accessed | tf_op | source)
XLA Modules:
  0.0 68.6 jit_solution(6289807288256892170)
XLA Ops:
  0.6 0.0 copy-start.3
  0.6 37.9 %shard_map.77 = (bf16[32,4,16,128]{3,2,1,0:T(8,128)(2,1)S(1)}, bf16[16,4,32,128]{3,2,1,0:T(8,128)(2,1)S(1)}) custom-call(s32[128]{0:T(128)} %prompts.3, bf16[2,16,4,512]{3,2,1,0:T(4,128)(2,1)} %raw_hbm.1), custom_call_target="tpu_custom_call" | custom-call | flops 1000000 | bytes 2000000 | tf_op jit(solution)/shard_map/pallas_call | solution.py:358
  38.6 0.0 copy-start.4
  38.6 0.0 copy-done.3
  38.6 0.6 copy-done.4
  39.2 0.0 copy-start.1
  39.3 1.0 %copy-done.1 = bf16[2,128,1024]{2,1,0:T(8,128)(2,1)S(1)} copy-done((bf16[2,128,1024]{2,1,0:T(8,128)(2,1)S(1)}, bf16[2,128,1024]{2,1,0:T(8,128)(2,1)}, u32[]{:S(2)}) %copy-start.1) | copy-done | bytes 524312
  40.3 0.0 copy-start.2
  40.3 1.0 %copy-done.2 = bf16[2,2,128,512]{3,2,1,0:T(8,128)(2,1)S(1)} copy-done((bf16[2,2,128,512]{3,2,1,0:T(8,128)(2,1)S(1)}, bf16[2,2,128,512]{3,2,1,0:T(8,128)(2,1)}, u32[]{:S(2)}) %copy-start.2) | copy-done | bytes 524312
  41.3 4.5 %shard_map.78 = (bf16[2,128,1024]{2,1,0:T(8,128)(2,1)}, f32[2,1,128]{2,1,0:T(1,128)S(1)}) custom-call(s32[2]{0:T(128)S(1)} %copy-done.4, f32[8,128]{1,0:T(8,128)S(1)} %bitcast.1, bf16[2,128,1024]{2,1,0:T(8,128)(2,1)S(1)} %copy-done.1, bf16[2,2,128,512]{3,2,1,0:T(8,128)(2,1)S(1)} %copy-done.2, bf16[32,4,16,128]{3,2,1,0:T(8,128)(2,1)S(1)} %get-tuple-element.6.all_a, ...), custom_call_target="tpu_custom_call" | custom-call | flops 700000000 | bytes 2000000 | tf_op jit(solution)/shard_map/pallas_call | solution.py:384
  45.9 0.0 copy-start
  45.9 0.6 copy-done
  46.4 21.0 %shard_map.79 = f32[2]{0:T(128)} custom-call(s32[128]{0:T(128)} %prompts.3, f32[2,1,128]{2,1,0:T(1,128)} %copy-done), custom_call_target="tpu_custom_call" | custom-call | flops 10000 | bytes 10000 | tf_op jit(solution)/shard_map/pallas_call | solution.py:404
  67.5 1.1 %copy.9 = f32[2]{0:T(128)} copy(f32[2]{0:T(128)} %shard_map.79) | data formatting | bytes 16
Async XLA Ops:
  0.6 38.0 %copy-start.3 = (f32[1024]{0:T(1024)S(1)}, f32[1024]{0:T(1024)}, u32[]{:S(2)}) copy-start(f32[1024]{0:T(1024)} %param.11) | copy-start | bytes 12292
  38.6 0.7 copy-start.4
  39.2 1.0 %copy-start.1 = (bf16[2,128,1024]{2,1,0:T(8,128)(2,1)S(1)}, bf16[2,128,1024]{2,1,0:T(8,128)(2,1)}, u32[]{:S(2)}) copy-start(bf16[2,128,1024]{2,1,0:T(8,128)(2,1)} %q.1) | copy-start | bytes 1572868
  40.3 1.0 %copy-start.2 = (bf16[2,2,128,512]{3,2,1,0:T(8,128)(2,1)S(1)}, bf16[2,2,128,512]{3,2,1,0:T(8,128)(2,1)}, u32[]{:S(2)}) copy-start(bf16[2,2,128,512]{3,2,1,0:T(8,128)(2,1)} %kv.1) | copy-start | bytes 1572868
  45.9 0.6 copy-start

commit v4 on v2

--- a/solution.py
+++ b/solution.py
@@ -14,11 +14,22 @@
 MESH = pl.DeviceIdType.MESH
 
 NZ, NX, NY, NT = 4, 4, 8, 4
-NXY, NZX, NZT = NX * NY, NZ * NX, NZ * NT
+NXY, NZX = NX * NY, NZ * NX
 PROMPTS = 16
 TOKENS = 4
 PIECES = 4
 ROWS = PIECES * TOKENS
+
+
+def far_first(first, second):
+    places = [(a, b) for a in range(first[0]) for b in range(second[0]) if (a, b) != (0, 0)]
+    hops = lambda n, step: min(n[0] - step, step) * n[1]
+    return sorted(places, key=lambda p: (-hops(first, p[0]) - hops(second, p[1]), p))
+
+
+FAR_XY = far_first((NX, 1), (NY, 1))
+FAR_ZX = far_first((NZ, 2), (NX, 1))
+FAR_ZT = far_first((NZ, 2), (NT, 1))
 
 
 def attention(scores_parts, values, scale2):
@@ -63,6 +74,7 @@
     all_b,
     row_1,
     row_2,
+    lines,
     load_sem,
     ring_send,
     ring_recv,
@@ -77,17 +89,17 @@
     y = lax.rem(xy, NY)
     zx = zh * NX + x
 
-    def at_xy(j):
-        return zh * NXY + j
-
-    def at_zx(j):
-        return j * NY + y
-
     def at_z(step):
         return lax.rem(zh + step, NZ) * NXY + xy
 
     def at_y(step):
         return zh * NXY + x * NY + lax.rem(y + step, NY)
+
+    def at_x(step):
+        return zh * NXY + lax.rem(x + step, NX) * NY + y
+
+    def at_tp(step):
+        return lax.rem(tp + step, NT)
 
     load_raw = pltpu.make_async_copy(raw_hbm, raw, load_sem.at[0])
     load_q = pltpu.make_async_copy(q_hbm, q, load_sem.at[1])
@@ -101,23 +113,14 @@
     def greet(device, tp_index):
         pl.semaphore_signal(barrier, inc=1, device_id=(device, tp_index), device_id_type=MESH)
 
-    def greet_xy(i, c):
-        greet(at_xy(lax.rem(xy + i, NXY)), tp)
-        return c
-
-    lax.fori_loop(1, NXY, greet_xy, 0)
-
-    def greet_zx(i, c):
-        greet(at_zx(lax.rem(zh + 1 + lax.div(i, NX), NZ) * NX + lax.rem(i, NX)), tp)
-        return c
-
-    lax.fori_loop(0, (NZ - 1) * NX, greet_zx, 0)
-
-    def greet_tp(i, c):
-        greet(lax.div(i, NT - 1) * NXY + xy, lax.rem(tp + 1 + lax.rem(i, NT - 1), NT))
-        return c
-
-    lax.fori_loop(0, NZ * (NT - 1), greet_tp, 0)
+    for i in range(1, NY):
+        greet(at_y(i), tp)
+    for i in range(1, NZ):
+        greet(at_z(i), tp)
+    for i in range(1, NX):
+        greet(at_x(i), tp)
+    for i in range(1, NT):
+        greet(me, at_tp(i))
 
     load_raw.wait()
 
@@ -135,7 +138,7 @@
 
     lax.fori_loop(0, PROMPTS, split, 0)
 
-    pl.semaphore_wait(barrier, (NXY - 1) + (NZ - 1) * NX + NZ * (NT - 1))
+    pl.semaphore_wait(barrier, (NY - 1) + (NZ - 1) + (NX - 1) + (NT - 1))
 
     half = PROMPTS // 2
     lo, hi = pl.ds(0, half), pl.ds(half, half)
@@ -168,6 +171,10 @@
     ]
     for copy in first:
         copy.start()
+    for i in range(1, NX):
+        pl.semaphore_signal(lines.at[0], inc=1, device_id=(at_x(i), tp), device_id_type=MESH)
+    for i in range(1, NZ):
+        pl.semaphore_signal(lines.at[1], inc=1, device_id=(at_z(i), tp), device_id_type=MESH)
     first[0].wait_recv()
     second[0].start()
     first[1].wait_recv()
@@ -197,53 +204,48 @@
 
         lax.fori_loop(0, PROMPTS // 4, four, 0)
 
-    def send(offsets_a, offsets_b):
-        places_a = [lax.rem(xy + i, NXY) for i in offsets_a]
-        places_b = [lax.rem(zx + i, NZX) for i in offsets_b]
-        blocks_b = [by_prompt_b[prompts[at_zx(j)]] for j in places_b]
-        blocks_a = [by_prompt_a[prompts[at_xy(j)]] for j in places_a]
-        for i, block in zip(offsets_b, blocks_b):
-            out_b[i] = block
-        for i, block in zip(offsets_a, blocks_a):
-            out_a[i] = block
-        for i, j in zip(offsets_b, places_b):
+    def beside_xy(dx, dy):
+        return zh * NXY + lax.rem(x + dx, NX) * NY + lax.rem(y + dy, NY)
+
+    def beside_zx(dz, dx):
+        return lax.rem(zh + dz, NZ) * NXY + lax.rem(x + dx, NX) * NY + y
+
+    def send(plan, slots, places, by_prompt, out, everyone, mine_at):
+        blocks = [by_prompt[prompts[j]] for j in places]
+        for i, block in zip(slots, blocks):
+            out[i] = block
+        for i, j in zip(slots, places):
             pltpu.make_async_remote_copy(
-                src_ref=out_b.at[i],
-                dst_ref=all_b.at[zx],
-                send_sem=send_sem.at[1],
-                recv_sem=recv_sem.at[1],
-                device_id=(at_zx(j), tp),
+                src_ref=out.at[i],
+                dst_ref=everyone.at[mine_at],
+                send_sem=send_sem.at[plan],
+                recv_sem=recv_sem.at[plan],
+                device_id=(j, tp),
                 device_id_type=MESH,
             ).start()
-        for i, j in zip(offsets_a, places_a):
-            pltpu.make_async_remote_copy(
-                src_ref=out_a.at[i],
-                dst_ref=all_a.at[xy],
-                send_sem=send_sem.at[0],
-                recv_sem=recv_sem.at[0],
-                device_id=(at_xy(j), tp),
-                device_id_type=MESH,
-            ).start()
+
+    def send_a(low, high):
+        places = [beside_xy(*offset) for offset in FAR_XY[low:high]]
+        send(0, range(low, high), places, by_prompt_a, out_a, all_a, xy)
+
+    def send_b(low, high):
+        places = [beside_zx(*offset) for offset in FAR_ZX[low:high]]
+        send(1, range(low, high), places, by_prompt_b, out_b, all_b, zx)
 
     regroup(own_a, got_a, NZ - 1, by_prompt_a)
-
-    def send_all_a(i, c):
-        send([6 * i + 1 + n for n in range(6)], [])
-        return c
-
-    lax.fori_loop(0, 5, send_all_a, 0)
-    send([NXY - 1], [])
+    pl.semaphore_wait(lines.at[0], NX - 1)
+    pl.semaphore_wait(lines.at[1], NZ - 1)
+
+    for low in range(0, NXY - 1, 6):
+        send_a(low, min(low + 6, NXY - 1))
     first[4].wait_recv()
     first[5].wait_recv()
     for copy in second[2:]:
         copy.wait_recv()
     regroup(own_b, got_b, NY - 1, by_prompt_b)
 
-    def send_all_b(i, c):
-        send([], [5 * i + 1 + n for n in range(5)])
-        return c
-
-    lax.fori_loop(0, 3, send_all_b, 0)
+    for low in range(0, NZX - 1, 5):
+        send_b(low, low + 5)
 
     mine = prompts[me]
     all_a[xy] = by_prompt_a[mine]
@@ -280,18 +282,36 @@
     def reward_of(g):
         k, v = keys_values(g)
         heads = (2 * g, 2 * g + 1)
+        rows = [
+            jnp.concatenate([last[:, h * HEAD_DIM : (h + 1) * HEAD_DIM] for h in heads], axis=0)
+            for last in last_q
+        ]
+        own, own_v = [], []
         for r in range(responses):
-            rows = jnp.concatenate(
-                [last_q[r][:, h * HEAD_DIM : (h + 1) * HEAD_DIM] for h in heads], axis=0
+            its_k, its_v = own_keys_values(r, g)
+            scores = scores_of(rows[r], its_k)
+            seen = lax.broadcasted_iota(jnp.int32, scores.shape, 1) < lengths[r]
+            own.append(jnp.where(seen, scores, -1e30))
+            own_v.append(its_v)
+        shared = scores_of(jnp.concatenate(rows, axis=0), k)
+        own = jnp.concatenate(own, axis=0)
+        top = jnp.maximum(
+            jnp.max(shared, axis=1, keepdims=True), jnp.max(own, axis=1, keepdims=True)
+        )
+        shared = jnp.exp2((shared - top) * scale2)
+        own = jnp.exp2((own - top) * scale2)
+        total = jnp.sum(shared, axis=1, keepdims=True) + jnp.sum(own, axis=1, keepdims=True)
+        own = own.astype(jnp.bfloat16)
+        mixed = jnp.dot(shared.astype(jnp.bfloat16), v, preferred_element_type=jnp.float32)
+        for r in range(responses):
+            low = 16 * r
+            part = mixed[low : low + 16] + jnp.dot(
+                own[low : low + 16], own_v[r], preferred_element_type=jnp.float32
             )
-            own_k, own_v = own_keys_values(r, g)
-            own = scores_of(rows, own_k)
-            seen = lax.broadcasted_iota(jnp.int32, own.shape, 1) < lengths[r]
-            own = jnp.where(seen, own, -1e30)
-            mixed = attention([scores_of(rows, k), own], [v, own_v], scale2)
-            mixed = mixed.astype(jnp.bfloat16).astype(jnp.float32)
+            part = part * (1.0 / total[low : low + 16])
+            part = part.astype(jnp.bfloat16).astype(jnp.float32)
             for n, h in enumerate(heads):
-                partial[r] = partial[r] + mixed[8 * n : 8 * n + 8] * probe[h : h + 1, :]
+                partial[r] = partial[r] + part[8 * n : 8 * n + 8] * probe[h : h + 1, :]
 
     def attend(r, g):
         k, v = keys_values(g)
@@ -329,42 +349,37 @@
         row = jnp.where(lane == PROMPTS + r, sums[r], row)
 
     zt = zh * NT + tp
-    row_1[zt] = row
-
-    for i in range(1, NZT):
-        j = lax.rem(zt + i, NZT)
-        pltpu.make_async_remote_copy(
-            src_ref=row_1.at[zt],
-            dst_ref=row_1.at[zt],
-            send_sem=send_sem.at[2],
-            recv_sem=recv_sem.at[2],
-            device_id=(lax.div(j, NT) * NXY + xy, lax.rem(j, NT)),
-            device_id_type=MESH,
-        ).start()
-
-    for r in range(responses):
-        attend(r, 2)
-
-    wait_bytes(row_1.at[pl.ds(0, NZT - 1)], recv_sem.at[2])
-    line = jnp.sum(row_1[...], axis=0)
+    rounds = (
+        (row_1, zt, [(at_z(dz), at_tp(dt)) for dz, dt in FAR_ZT]),
+        (row_2, xy, [(beside_xy(*offset), tp) for offset in FAR_XY]),
+    )
+
+    def send_row(n, row):
+        ref, slot, devices = rounds[n]
+        ref[slot] = row
+        for device in devices:
+            pltpu.make_async_remote_copy(
+                src_ref=ref.at[slot],
+                dst_ref=ref.at[slot],
+                send_sem=send_sem.at[2 + n],
+                recv_sem=recv_sem.at[2 + n],
+                device_id=device,
+                device_id_type=MESH,
+            ).start()
+
+    def wait_rows(n):
+        ref, _, devices = rounds[n]
+        wait_bytes(ref.at[pl.ds(0, len(devices))], recv_sem.at[2 + n])
+
+    send_row(0, row)
+    attend(0, 2)
+    attend(1, 2)
+    wait_rows(0)
     rewards = jnp.sum(row_1[pl.ds(zh * NT, NT)], axis=0)
-    row_2[xy] = line
-
-    for i in range(1, NXY):
-        j = lax.rem(xy + i, NXY)
-        pltpu.make_async_remote_copy(
-            src_ref=row_2.at[xy],
-            dst_ref=row_2.at[xy],
-            send_sem=send_sem.at[3],
-            recv_sem=recv_sem.at[3],
-            device_id=(at_xy(j), tp),
-            device_id_type=MESH,
-        ).start()
-
-    for r in range(responses):
-        attend(r, 3)
-
-    wait_bytes(row_2.at[pl.ds(0, NXY - 1)], recv_sem.at[3])
+    send_row(1, jnp.sum(row_1[...], axis=0))
+    attend(0, 3)
+    attend(1, 3)
+    wait_rows(1)
     table = jnp.sum(row_2[...], axis=0)
     group = jnp.sum(jnp.where(lane == mine, table, 0.0), axis=1, keepdims=True) / BEST
     result = rewards - group
@@ -375,10 +390,10 @@
         copy.wait_send()
     for copy in second:
         copy.wait_send()
-    wait_bytes(out_a.at[pl.ds(1, NXY - 1)], send_sem.at[0])
-    wait_bytes(out_b.at[pl.ds(1, NZX - 1)], send_sem.at[1])
-    wait_bytes(row_1.at[pl.ds(0, NZT - 1)], send_sem.at[2])
-    wait_bytes(row_2.at[pl.ds(0, NXY - 1)], send_sem.at[3])
+    wait_bytes(out_a.at[pl.ds(0, NXY - 1)], send_sem.at[0])
+    wait_bytes(out_b.at[pl.ds(0, NZX - 1)], send_sem.at[1])
+    for n, (ref, _, devices) in enumerate(rounds):
+        wait_bytes(ref.at[pl.ds(0, len(devices))], send_sem.at[2 + n])
 
 
 def shards(response_queries, response_kv, prompt_kv, response_lengths, device_prompt, probe_weight):
@@ -410,8 +425,9 @@
             pltpu.VMEM((NZX, PIECES, NY * TOKENS, HEAD_DIM), bf16),
             pltpu.VMEM((NXY, PIECES, NZ * TOKENS, HEAD_DIM), bf16),
             pltpu.VMEM((NZX, PIECES, NY * TOKENS, HEAD_DIM), bf16),
-            pltpu.VMEM((NZT, 1, HEAD_DIM), jnp.float32),
+            pltpu.VMEM((NZ * NT, 1, HEAD_DIM), jnp.float32),
             pltpu.VMEM((NXY, 1, HEAD_DIM), jnp.float32),
+            pltpu.SemaphoreType.REGULAR((2,)),
             pltpu.SemaphoreType.DMA((3,)),
             pltpu.SemaphoreType.DMA((12,)),
             pltpu.SemaphoreType.DMA((12,)),

time: 57.9 us -> 53.2 us (0.919)
  Pallas kernels: 55.8 us -> 51 us
    pallas_call x1, Pallas kernels: 55.8 us -> 51 us  [shards(): pl.pallas_call(kernel, out_shape=(pltpu.VMEM(response_queries.shape, bf16...]
where the time goes in v4:
time: 53.2 us; the launch traced here: 53 us
  Pallas kernels  51 us (96%)
  local copies, waits for them, and re-layouts  1.31 us (2%)
  between operations  0.64 us (1%)
    pallas_call x1, Pallas kernels, shards(): pl.pallas_call(kernel, out_shape=(pltpu.VMEM(response_queries.shape, bf16...  51 us
    unnamed x2, local copies, waits for them, and re-layouts  1.31 us

profile of v4, /device:TPU:1, one launch (start us, length us, event | category | flops | bytes accessed | tf_op | source)
XLA Modules:
  0.0 53.0 jit_solution(15690890709621389108)
XLA Ops:
  0.6 51.0 %shard_map.77 = (bf16[2,128,1024]{2,1,0:T(8,128)(2,1)S(1)}, f32[2]{0:T(128)S(1)}) custom-call(s32[2]{0:T(128)} %lengths.1, s32[128]{0:T(128)} %prompts.1, f32[8,128]{1,0:T(8,128)} %bitcast.1, bf16[2,128,1024]{2,1,0:T(8,128)(2,1)} %q_hbm.1, bf16[2,2,128,512]{3,2,1,0:T(8,128)(2,1)} %kv_hbm.1, bf16[2,16,4,512]{3,2,1,0:T(4,128)(2,1)} %raw_hbm.1), custom_call_target="tpu_custom_call" | custom-call | flops 700000000 | bytes 2000000 | tf_op jit(solution)/shard_map/pallas_call | solution.py:406
  51.7 0.8 %copy.10 = bf16[2,128,1024]{2,1,0:T(8,128)(2,1)} copy(bf16[2,128,1024]{2,1,0:T(8,128)(2,1)S(1)} %get-tuple-element.2) | data formatting | bytes 1048576
  52.5 0.5 copy.11

commit v5 on v4

--- a/solution.py
+++ b/solution.py
@@ -113,13 +113,13 @@
     def greet(device, tp_index):
         pl.semaphore_signal(barrier, inc=1, device_id=(device, tp_index), device_id_type=MESH)
 
-    for i in range(1, NY):
+    for i in (4, 3, 5, 2, 6, 1, 7):
         greet(at_y(i), tp)
-    for i in range(1, NZ):
+    for i in (2, 1, 3):
         greet(at_z(i), tp)
-    for i in range(1, NX):
+    for i in (2, 1, 3):
         greet(at_x(i), tp)
-    for i in range(1, NT):
+    for i in (2, 3, 1):
         greet(me, at_tp(i))
 
     load_raw.wait()
@@ -169,22 +169,22 @@
         ring(10, got_b.at[3, hi], got_b.at[6, hi], at_y(NY - 2)),
         ring(11, got_b.at[3], got_b.at[5], at_y(NY - 1)),
     ]
-    for copy in first:
-        copy.start()
+    for n in (2, 3, 0, 1, 4, 5):
+        first[n].start()
     for i in range(1, NX):
         pl.semaphore_signal(lines.at[0], inc=1, device_id=(at_x(i), tp), device_id_type=MESH)
     for i in range(1, NZ):
         pl.semaphore_signal(lines.at[1], inc=1, device_id=(at_z(i), tp), device_id_type=MESH)
-    first[0].wait_recv()
-    second[0].start()
-    first[1].wait_recv()
-    second[1].start()
     first[2].wait_recv()
     second[2].start()
     second[3].start()
     first[3].wait_recv()
     second[4].start()
     second[5].start()
+    first[0].wait_recv()
+    second[0].start()
+    first[1].wait_recv()
+    second[1].start()
     second[0].wait_recv()
     second[1].wait_recv()
 
@@ -236,8 +236,8 @@
     pl.semaphore_wait(lines.at[0], NX - 1)
     pl.semaphore_wait(lines.at[1], NZ - 1)
 
-    for low in range(0, NXY - 1, 6):
-        send_a(low, min(low + 6, NXY - 1))
+    for low in range(0, NXY // 2, 4):
+        send_a(low, low + 4)
     first[4].wait_recv()
     first[5].wait_recv()
     for copy in second[2:]:
@@ -246,6 +246,8 @@
 
     for low in range(0, NZX - 1, 5):
         send_b(low, low + 5)
+    for low in range(NXY // 2, NXY - 1, 5):
+        send_a(low, low + 5)
 
     mine = prompts[me]
     all_a[xy] = by_prompt_a[mine]
@@ -334,9 +336,6 @@
     wait_bytes(all_a.at[pl.ds(0, NXY - 1)], recv_sem.at[0])
     for g in range(2):
         reward_of(g)
-    for g in range(2):
-        for r in range(responses):
-            attend(r, g)
 
     wait_bytes(all_b.at[pl.ds(0, NZX - 1)], recv_sem.at[1])
     for g in range(2, kv_heads):
@@ -372,13 +371,15 @@
         wait_bytes(ref.at[pl.ds(0, len(devices))], recv_sem.at[2 + n])
 
     send_row(0, row)
-    attend(0, 2)
-    attend(1, 2)
+    for g in range(2):
+        for r in range(responses):
+            attend(r, g)
     wait_rows(0)
     rewards = jnp.sum(row_1[pl.ds(zh * NT, NT)], axis=0)
     send_row(1, jnp.sum(row_1[...], axis=0))
-    attend(0, 3)
-    attend(1, 3)
+    for g in range(2, kv_heads):
+        for r in range(responses):
+            attend(r, g)
     wait_rows(1)
     table = jnp.sum(row_2[...], axis=0)
     group = jnp.sum(jnp.where(lane == mine, table, 0.0), axis=1, keepdims=True) / BEST

time: 53.2 us -> 52.5 us (0.987)
  Pallas kernels: 51 us -> 50.4 us
    pallas_call x1, Pallas kernels: 51 us -> 50.4 us  [shards(): pl.pallas_call(kernel, out_shape=(pltpu.VMEM(response_queries.shape, bf16...]
where the time goes in v5:
time: 52.5 us; the launch traced here: 52.4 us
  Pallas kernels  50.4 us (96%)
  local copies, waits for them, and re-layouts  1.31 us (2%)
  between operations  0.64 us (1%)
    pallas_call x1, Pallas kernels, shards(): pl.pallas_call(kernel, out_shape=(pltpu.VMEM(response_queries.shape, bf16...  50.4 us
    unnamed x2, local copies, waits for them, and re-layouts  1.31 us

profile of v5, /device:TPU:1, one launch (start us, length us, event | category | flops | bytes accessed | tf_op | source)
XLA Modules:
  0.0 52.4 jit_solution(6580726523104787184)
XLA Ops:
  0.6 50.4 %shard_map.77 = (bf16[2,128,1024]{2,1,0:T(8,128)(2,1)S(1)}, f32[2]{0:T(128)S(1)}) custom-call(s32[2]{0:T(128)} %lengths.1, s32[128]{0:T(128)} %prompts.1, f32[8,128]{1,0:T(8,128)} %bitcast.1, bf16[2,128,1024]{2,1,0:T(8,128)(2,1)} %q_hbm.1, bf16[2,2,128,512]{3,2,1,0:T(8,128)(2,1)} %kv_hbm.1, bf16[2,16,4,512]{3,2,1,0:T(4,128)(2,1)} %raw_hbm.1), custom_call_target="tpu_custom_call" | custom-call | flops 700000000 | bytes 2000000 | tf_op jit(solution)/shard_map/pallas_call | solution.py:407
  51.1 0.8 %copy.10 = bf16[2,128,1024]{2,1,0:T(8,128)(2,1)} copy(bf16[2,128,1024]{2,1,0:T(8,128)(2,1)S(1)} %get-tuple-element.2) | data formatting | bytes 1048576
  51.9 0.5 copy.11

commit v6 on v5

--- a/solution.py
+++ b/solution.py
@@ -51,14 +51,17 @@
 
 
 def kernel(
-    lengths,
-    prompts,
-    probe,
+    lengths_hbm,
+    prompts_hbm,
+    probe_hbm,
     q_hbm,
     kv_hbm,
     raw_hbm,
     context,
     advantage,
+    lengths,
+    prompts,
+    probe,
     q,
     kv,
     raw,
@@ -101,13 +104,6 @@
     def at_tp(step):
         return lax.rem(tp + step, NT)
 
-    load_raw = pltpu.make_async_copy(raw_hbm, raw, load_sem.at[0])
-    load_q = pltpu.make_async_copy(q_hbm, q, load_sem.at[1])
-    load_kv = pltpu.make_async_copy(kv_hbm, kv, load_sem.at[2])
-    load_raw.start()
-    load_q.start()
-    load_kv.start()
-
     barrier = pltpu.get_barrier_semaphore()
 
     def greet(device, tp_index):
@@ -121,6 +117,19 @@
         greet(at_x(i), tp)
     for i in (2, 3, 1):
         greet(me, at_tp(i))
+
+    load_raw = pltpu.make_async_copy(raw_hbm, raw, load_sem.at[0])
+    load_prompts = pltpu.make_async_copy(prompts_hbm, prompts, load_sem.at[1])
+    load_rest = [
+        pltpu.make_async_copy(src, dst, load_sem.at[2 + n])
+        for n, (src, dst) in enumerate(
+            ((q_hbm, q), (kv_hbm, kv), (lengths_hbm, lengths), (probe_hbm, probe))
+        )
+    ]
+    load_raw.start()
+    load_prompts.start()
+    for load in load_rest:
+        load.start()
 
     load_raw.wait()
 
@@ -233,6 +242,7 @@
         send(1, range(low, high), places, by_prompt_b, out_b, all_b, zx)
 
     regroup(own_a, got_a, NZ - 1, by_prompt_a)
+    load_prompts.wait()
     pl.semaphore_wait(lines.at[0], NX - 1)
     pl.semaphore_wait(lines.at[1], NZ - 1)
 
@@ -253,8 +263,8 @@
     all_a[xy] = by_prompt_a[mine]
     all_b[zx] = by_prompt_b[mine]
 
-    load_q.wait()
-    load_kv.wait()
+    for load in load_rest:
+        load.wait()
     responses, steps, width = q.shape
     scale2 = math.log2(math.e) / math.sqrt(SCALAR)
     kv_heads = kv.shape[3] // HEAD_DIM
@@ -383,9 +393,7 @@
     wait_rows(1)
     table = jnp.sum(row_2[...], axis=0)
     group = jnp.sum(jnp.where(lane == mine, table, 0.0), axis=1, keepdims=True) / BEST
-    result = rewards - group
-    for r in range(responses):
-        advantage[r] = jnp.sum(jnp.where(lane == PROMPTS + r, result, 0.0))
+    advantage[...] = rewards - group
 
     for copy in first:
         copy.wait_send()
@@ -399,7 +407,6 @@
 
 def shards(response_queries, response_kv, prompt_kv, response_lengths, device_prompt, probe_weight):
     bf16 = jnp.bfloat16
-    smem = pl.BlockSpec(memory_space=pltpu.SMEM)
     vmem = pl.BlockSpec(memory_space=pltpu.VMEM)
     anywhere = pl.BlockSpec(memory_space=pl.ANY)
     in_hbm = functools.partial(pltpu.with_memory_space_constraint, memory_space=pltpu.HBM)
@@ -408,11 +415,14 @@
         kernel,
         out_shape=(
             pltpu.VMEM(response_queries.shape, bf16),
-            jax.ShapeDtypeStruct(response_lengths.shape, jnp.float32),
+            pltpu.VMEM((1, HEAD_DIM), jnp.float32),
         ),
-        in_specs=[smem, smem, vmem, anywhere, anywhere, anywhere],
-        out_specs=(vmem, smem),
+        in_specs=[anywhere] * 6,
+        out_specs=(vmem, vmem),
         scratch_shapes=[
+            pltpu.SMEM(response_lengths.shape, jnp.int32),
+            pltpu.SMEM(device_prompt.shape, jnp.int32),
+            pltpu.VMEM((probe_weight.shape[0] // HEAD_DIM, HEAD_DIM), jnp.float32),
             pltpu.VMEM(response_queries.shape, bf16),
             pltpu.VMEM(response_kv.shape, bf16),
             pltpu.VMEM(prompt_kv.shape, bf16),
@@ -429,7 +439,7 @@
             pltpu.VMEM((NZ * NT, 1, HEAD_DIM), jnp.float32),
             pltpu.VMEM((NXY, 1, HEAD_DIM), jnp.float32),
             pltpu.SemaphoreType.REGULAR((2,)),
-            pltpu.SemaphoreType.DMA((3,)),
+            pltpu.SemaphoreType.DMA((6,)),
             pltpu.SemaphoreType.DMA((12,)),
             pltpu.SemaphoreType.DMA((12,)),
             pltpu.SemaphoreType.DMA((4,)),
@@ -449,7 +459,7 @@
         in_hbm(response_kv),
         in_hbm(prompt_kv),
     )
-    return context, advantage
+    return context, advantage[0, PROMPTS : PROMPTS + response_lengths.shape[0]]
 
 
 def solution(mesh):

time: 52.5 us -> 51.2 us (0.975)
  Pallas kernels: 50.4 us -> 49 us
    pallas_call x1, Pallas kernels: 50.4 us -> 49 us  [shards(): pl.pallas_call(kernel, out_shape=(pltpu.VMEM(response_queries.shape, bf16...]
    squeeze x0 -> x1, local copies, waits for them, and re-layouts: none -> 0.58 us  [shards(): return (context, advantage[0, PROMPTS:PROMPTS + response_lengths.shape[0]])]
    unnamed x2 -> x1, local copies, waits for them, and re-layouts: 1.31 us -> 0.8 us
where the time goes in v6:
time: 51.2 us; the launch traced here: 51.1 us
  Pallas kernels  49 us (96%)
  local copies, waits for them, and re-layouts  1.38 us (3%)
  between operations  0.64 us (1%)
    pallas_call x1, Pallas kernels, shards(): pl.pallas_call(kernel, out_shape=(pltpu.VMEM(response_queries.shape, bf16...  49 us

profile of v6, /device:TPU:1, one launch (start us, length us, event | category | flops | bytes accessed | tf_op | source)
XLA Modules:
  0.0 51.1 jit_solution(16124091091576830793)
XLA Ops:
  0.6 49.0 %shard_map.77 = (bf16[2,128,1024]{2,1,0:T(8,128)(2,1)S(1)}, f32[1,128]{1,0:T(1,128)S(1)}) custom-call(s32[2]{0:T(128)} %lengths_hbm.1, s32[128]{0:T(128)} %prompts_hbm.1, f32[8,128]{1,0:T(8,128)} %bitcast.3, bf16[2,128,1024]{2,1,0:T(8,128)(2,1)} %q_hbm.1, bf16[2,2,128,512]{3,2,1,0:T(8,128)(2,1)} %kv_hbm.1, bf16[2,16,4,512]{3,2,1,0:T(4,128)(2,1)} %raw_hbm.1), custom_call_target="tpu_custom_call" | custom-call | flops 700000000 | bytes 2000000 | tf_op jit(solution)/shard_map/pallas_call | solution.py:414
  49.7 0.8 %copy.9 = bf16[2,128,1024]{2,1,0:T(8,128)(2,1)} copy(bf16[2,128,1024]{2,1,0:T(8,128)(2,1)S(1)} %get-tuple-element.6) | data formatting | bytes 1048576
  50.5 0.6 %slice_bitcast_fusion = f32[2]{0:T(128)} fusion(f32[1,128]{1,0:T(1,128)S(1)} %get-tuple-element.5), kind=kLoop, calls=%fused_computation | loop fusion | bytes 16 | tf_op jit(solution)/shard_map/squeeze | solution.py:462

commit v7 on v6

--- a/solution.py
+++ b/solution.py
@@ -109,9 +109,9 @@
     def greet(device, tp_index):
         pl.semaphore_signal(barrier, inc=1, device_id=(device, tp_index), device_id_type=MESH)
 
-    for i in (4, 3, 5, 2, 6, 1, 7):
+    for i in (2, 6, 1, 7):
         greet(at_y(i), tp)
-    for i in (2, 1, 3):
+    for i in (1, 3):
         greet(at_z(i), tp)
     for i in (2, 1, 3):
         greet(at_x(i), tp)
@@ -147,7 +147,7 @@
 
     lax.fori_loop(0, PROMPTS, split, 0)
 
-    pl.semaphore_wait(barrier, (NY - 1) + (NZ - 1) + (NX - 1) + (NT - 1))
+    pl.semaphore_wait(barrier, 4 + 2 + (NX - 1) + (NT - 1))
 
     half = PROMPTS // 2
     lo, hi = pl.ds(0, half), pl.ds(half, half)
@@ -180,6 +180,9 @@
     ]
     for n in (2, 3, 0, 1, 4, 5):
         first[n].start()
+    for device in (at_y(2), at_y(NY - 2), at_z(NZ - 1)):
+        pl.semaphore_signal(lines.at[2], inc=1, device_id=(device, tp), device_id_type=MESH)
+    pl.semaphore_wait(lines.at[2], 3)
     for i in range(1, NX):
         pl.semaphore_signal(lines.at[0], inc=1, device_id=(at_x(i), tp), device_id_type=MESH)
     for i in range(1, NZ):
@@ -438,7 +441,7 @@
             pltpu.VMEM((NZX, PIECES, NY * TOKENS, HEAD_DIM), bf16),
             pltpu.VMEM((NZ * NT, 1, HEAD_DIM), jnp.float32),
             pltpu.VMEM((NXY, 1, HEAD_DIM), jnp.float32),
-            pltpu.SemaphoreType.REGULAR((2,)),
+            pltpu.SemaphoreType.REGULAR((3,)),
             pltpu.SemaphoreType.DMA((6,)),
             pltpu.SemaphoreType.DMA((12,)),
             pltpu.SemaphoreType.DMA((12,)),

time: 51.2 us -> 50.5 us (0.986)
  Pallas kernels: 49 us -> 48.3 us
    pallas_call x1, Pallas kernels: 49 us -> 48.3 us  [shards(): pl.pallas_call(kernel, out_shape=(pltpu.VMEM(response_queries.shape, bf16...]
where the time goes in v7:
time: 50.5 us; the launch traced here: 50.4 us
  Pallas kernels  48.3 us (96%)
  local copies, waits for them, and re-layouts  1.38 us (3%)
  between operations  0.64 us (1%)
    pallas_call x1, Pallas kernels, shards(): pl.pallas_call(kernel, out_shape=(pltpu.VMEM(response_queries.shape, bf16...  48.3 us

profile of v7, /device:TPU:1, one launch (start us, length us, event | category | flops | bytes accessed | tf_op | source)
XLA Modules:
  0.0 50.4 jit_solution(17943265266166240975)
XLA Ops:
  0.6 48.3 %shard_map.77 = (bf16[2,128,1024]{2,1,0:T(8,128)(2,1)S(1)}, f32[1,128]{1,0:T(1,128)S(1)}) custom-call(s32[2]{0:T(128)} %lengths_hbm.1, s32[128]{0:T(128)} %prompts_hbm.1, f32[8,128]{1,0:T(8,128)} %bitcast.3, bf16[2,128,1024]{2,1,0:T(8,128)(2,1)} %q_hbm.1, bf16[2,2,128,512]{3,2,1,0:T(8,128)(2,1)} %kv_hbm.1, bf16[2,16,4,512]{3,2,1,0:T(4,128)(2,1)} %raw_hbm.1), custom_call_target="tpu_custom_call" | custom-call | flops 700000000 | bytes 2000000 | tf_op jit(solution)/shard_map/pallas_call | solution.py:417
  49.0 0.8 %copy.9 = bf16[2,128,1024]{2,1,0:T(8,128)(2,1)} copy(bf16[2,128,1024]{2,1,0:T(8,128)(2,1)S(1)} %get-tuple-element.6) | data formatting | bytes 1048576
  49.8 0.6 %slice_bitcast_fusion = f32[2]{0:T(128)} fusion(f32[1,128]{1,0:T(1,128)S(1)} %get-tuple-element.5), kind=kLoop, calls=%fused_computation | loop fusion | bytes 16 | tf_op jit(solution)/shard_map/squeeze | solution.py:465

commit v8 on v7

--- a/solution.py
+++ b/solution.py
@@ -28,7 +28,7 @@
 
 
 FAR_XY = far_first((NX, 1), (NY, 1))
-FAR_ZX = far_first((NZ, 2), (NX, 1))
+FAR_ZX = [p for p in far_first((NZ, 2), (NX, 1)) if p[0] != 2]
 FAR_ZT = far_first((NZ, 2), (NT, 1))
 
 
@@ -73,11 +73,15 @@
     by_prompt_b,
     out_a,
     out_b,
+    out_relay,
+    got_relay,
     all_a,
     all_b,
     row_1,
     row_2,
     lines,
+    relay_send,
+    relay_recv,
     load_sem,
     ring_send,
     ring_recv,
@@ -197,16 +201,13 @@
     second[0].start()
     first[1].wait_recv()
     second[1].start()
-    second[0].wait_recv()
-    second[1].wait_recv()
-
-    def regroup(own, got, slots, dst):
+
+    def regroup(tiles_of, dst, low):
         def one(p, c):
-            tiles = [own[p]] + [got[s, p] for s in range(slots)]
-            tiles = [t.astype(jnp.float32) for t in tiles]
+            tiles = [t.astype(jnp.float32) for t in tiles_of(p)]
             for g in range(PIECES):
                 rows = [t[TOKENS * g : TOKENS * (g + 1)] for t in tiles]
-                dst[p, g] = jnp.concatenate(rows, axis=0).astype(jnp.bfloat16)
+                dst[p, g, low : low + ROWS] = jnp.concatenate(rows, axis=0).astype(jnp.bfloat16)
             return c
 
         def four(i, c):
@@ -244,23 +245,56 @@
         places = [beside_zx(*offset) for offset in FAR_ZX[low:high]]
         send(1, range(low, high), places, by_prompt_b, out_b, all_b, zx)
 
-    regroup(own_a, got_a, NZ - 1, by_prompt_a)
+    first[4].wait_recv()
+    first[5].wait_recv()
+    regroup(lambda p: [own_b[p], got_b[0, p], got_b[1, p], got_b[2, p]], by_prompt_b, 0)
+    second[0].wait_recv()
+    second[1].wait_recv()
+    regroup(lambda p: [own_a[p], got_a[0, p], got_a[1, p], got_a[2, p]], by_prompt_a, 0)
     load_prompts.wait()
     pl.semaphore_wait(lines.at[0], NX - 1)
     pl.semaphore_wait(lines.at[1], NZ - 1)
 
     for low in range(0, NXY // 2, 4):
         send_a(low, low + 4)
-    first[4].wait_recv()
-    first[5].wait_recv()
     for copy in second[2:]:
         copy.wait_recv()
-    regroup(own_b, got_b, NY - 1, by_prompt_b)
-
-    for low in range(0, NZX - 1, 5):
-        send_b(low, low + 5)
+    regroup(lambda p: [got_b[s, p] for s in (3, 4, 5, 6)], by_prompt_b, ROWS)
+
+    for dx in range(NX):
+        block = by_prompt_b[prompts[beside_zx(2, dx)]]
+        out_relay[0, dx] = block[:2]
+        out_relay[1, dx] = block[2:]
+    relays = [
+        pltpu.make_async_remote_copy(
+            src_ref=out_relay.at[way],
+            dst_ref=got_relay.at[way],
+            send_sem=relay_send.at[way],
+            recv_sem=relay_recv.at[way],
+            device_id=(at_z(step), tp),
+            device_id_type=MESH,
+        )
+        for way, step in ((0, 1), (1, NZ - 1))
+    ]
+    for copy in relays:
+        copy.start()
+    send_b(0, 6)
+    send_b(6, len(FAR_ZX))
     for low in range(NXY // 2, NXY - 1, 5):
         send_a(low, low + 5)
+
+    for way, step in ((0, 1), (1, NZ - 1)):
+        relays[way].wait_recv()
+        origin = lax.rem(zh + NZ - step, NZ) * NX + x
+        for dx in (2, 1, 3, 0):
+            pltpu.make_async_remote_copy(
+                src_ref=got_relay.at[way, dx],
+                dst_ref=all_b.at[origin, pl.ds(2 * way, 2)],
+                send_sem=send_sem.at[1],
+                recv_sem=recv_sem.at[1],
+                device_id=(beside_zx(step, dx), tp),
+                device_id_type=MESH,
+            ).start()
 
     mine = prompts[me]
     all_a[xy] = by_prompt_a[mine]
@@ -384,15 +418,14 @@
         wait_bytes(ref.at[pl.ds(0, len(devices))], recv_sem.at[2 + n])
 
     send_row(0, row)
-    for g in range(2):
-        for r in range(responses):
-            attend(r, g)
+    order = [(r, g) for g in range(kv_heads) for r in range(responses)]
+    for r, g in order[:3]:
+        attend(r, g)
     wait_rows(0)
     rewards = jnp.sum(row_1[pl.ds(zh * NT, NT)], axis=0)
     send_row(1, jnp.sum(row_1[...], axis=0))
-    for g in range(2, kv_heads):
-        for r in range(responses):
-            attend(r, g)
+    for r, g in order[3:]:
+        attend(r, g)
     wait_rows(1)
     table = jnp.sum(row_2[...], axis=0)
     group = jnp.sum(jnp.where(lane == mine, table, 0.0), axis=1, keepdims=True) / BEST
@@ -400,7 +433,7 @@
 
     for copy in first:
         copy.wait_send()
-    for copy in second:
+    for copy in second + relays:
         copy.wait_send()
     wait_bytes(out_a.at[pl.ds(0, NXY - 1)], send_sem.at[0])
     wait_bytes(out_b.at[pl.ds(0, NZX - 1)], send_sem.at[1])
@@ -437,11 +470,15 @@
             pltpu.VMEM((PROMPTS, PIECES, NY * TOKENS, HEAD_DIM), bf16),
             pltpu.VMEM((NXY, PIECES, NZ * TOKENS, HEAD_DIM), bf16),
             pltpu.VMEM((NZX, PIECES, NY * TOKENS, HEAD_DIM), bf16),
+            pltpu.VMEM((2, NX, PIECES // 2, NY * TOKENS, HEAD_DIM), bf16),
+            pltpu.VMEM((2, NX, PIECES // 2, NY * TOKENS, HEAD_DIM), bf16),
             pltpu.VMEM((NXY, PIECES, NZ * TOKENS, HEAD_DIM), bf16),
             pltpu.VMEM((NZX, PIECES, NY * TOKENS, HEAD_DIM), bf16),
             pltpu.VMEM((NZ * NT, 1, HEAD_DIM), jnp.float32),
             pltpu.VMEM((NXY, 1, HEAD_DIM), jnp.float32),
             pltpu.SemaphoreType.REGULAR((3,)),
+            pltpu.SemaphoreType.DMA((2,)),
+            pltpu.SemaphoreType.DMA((2,)),
             pltpu.SemaphoreType.DMA((6,)),
             pltpu.SemaphoreType.DMA((12,)),
             pltpu.SemaphoreType.DMA((12,)),

time: 50.5 us -> 52.7 us (1.044)
  Pallas kernels: 48.3 us -> 50.5 us
    pallas_call x1, Pallas kernels: 48.3 us -> 50.5 us  [shards(): pl.pallas_call(kernel, out_shape=(pltpu.VMEM(response_queries.shape, bf16...]
where the time goes in v8:
time: 52.7 us; the launch traced here: 52.5 us
  Pallas kernels  50.5 us (96%)
  local copies, waits for them, and re-layouts  1.38 us (3%)
  between operations  0.64 us (1%)
    pallas_call x1, Pallas kernels, shards(): pl.pallas_call(kernel, out_shape=(pltpu.VMEM(response_queries.shape, bf16...  50.5 us

profile of v8, /device:TPU:1, one launch (start us, length us, event | category | flops | bytes accessed | tf_op | source)
XLA Modules:
  0.0 52.5 jit_solution(16179663814186812740)
XLA Ops:
  0.6 50.5 %shard_map.77 = (bf16[2,128,1024]{2,1,0:T(8,128)(2,1)S(1)}, f32[1,128]{1,0:T(1,128)S(1)}) custom-call(s32[2]{0:T(128)} %lengths_hbm.1, s32[128]{0:T(128)} %prompts_hbm.1, f32[8,128]{1,0:T(8,128)} %bitcast.3, bf16[2,128,1024]{2,1,0:T(8,128)(2,1)} %q_hbm.1, bf16[2,2,128,512]{3,2,1,0:T(8,128)(2,1)} %kv_hbm.1, bf16[2,16,4,512]{3,2,1,0:T(4,128)(2,1)} %raw_hbm.1), custom_call_target="tpu_custom_call" | custom-call | flops 700000000 | bytes 2000000 | tf_op jit(solution)/shard_map/pallas_call | solution.py:450
  51.2 0.8 %copy.9 = bf16[2,128,1024]{2,1,0:T(8,128)(2,1)} copy(bf16[2,128,1024]{2,1,0:T(8,128)(2,1)S(1)} %get-tuple-element.6) | data formatting | bytes 1048576
  52.0 0.6 %slice_bitcast_fusion = f32[2]{0:T(128)} fusion(f32[1,128]{1,0:T(1,128)S(1)} %get-tuple-element.5), kind=kLoop, calls=%fused_computation | loop fusion | bytes 16 | tf_op jit(solution)/shard_map/squeeze | solution.py:502

commit v9 on v7

--- a/solution.py
+++ b/solution.py
@@ -197,16 +197,13 @@
     second[0].start()
     first[1].wait_recv()
     second[1].start()
-    second[0].wait_recv()
-    second[1].wait_recv()
-
-    def regroup(own, got, slots, dst):
+
+    def regroup(tiles_of, dst, low):
         def one(p, c):
-            tiles = [own[p]] + [got[s, p] for s in range(slots)]
-            tiles = [t.astype(jnp.float32) for t in tiles]
+            tiles = [t.astype(jnp.float32) for t in tiles_of(p)]
             for g in range(PIECES):
                 rows = [t[TOKENS * g : TOKENS * (g + 1)] for t in tiles]
-                dst[p, g] = jnp.concatenate(rows, axis=0).astype(jnp.bfloat16)
+                dst[p, g, low : low + ROWS] = jnp.concatenate(rows, axis=0).astype(jnp.bfloat16)
             return c
 
         def four(i, c):
@@ -244,18 +241,21 @@
         places = [beside_zx(*offset) for offset in FAR_ZX[low:high]]
         send(1, range(low, high), places, by_prompt_b, out_b, all_b, zx)
 
-    regroup(own_a, got_a, NZ - 1, by_prompt_a)
+    first[4].wait_recv()
+    first[5].wait_recv()
+    regroup(lambda p: [own_b[p], got_b[0, p], got_b[1, p], got_b[2, p]], by_prompt_b, 0)
     load_prompts.wait()
     pl.semaphore_wait(lines.at[0], NX - 1)
     pl.semaphore_wait(lines.at[1], NZ - 1)
+    second[0].wait_recv()
+    second[1].wait_recv()
+    regroup(lambda p: [own_a[p], got_a[0, p], got_a[1, p], got_a[2, p]], by_prompt_a, 0)
 
     for low in range(0, NXY // 2, 4):
         send_a(low, low + 4)
-    first[4].wait_recv()
-    first[5].wait_recv()
     for copy in second[2:]:
         copy.wait_recv()
-    regroup(own_b, got_b, NY - 1, by_prompt_b)
+    regroup(lambda p: [got_b[s, p] for s in (3, 4, 5, 6)], by_prompt_b, ROWS)
 
     for low in range(0, NZX - 1, 5):
         send_b(low, low + 5)
@@ -384,15 +384,14 @@
         wait_bytes(ref.at[pl.ds(0, len(devices))], recv_sem.at[2 + n])
 
     send_row(0, row)
-    for g in range(2):
-        for r in range(responses):
-            attend(r, g)
+    order = [(r, g) for g in range(kv_heads) for r in range(responses)]
+    for r, g in order[:3]:
+        attend(r, g)
     wait_rows(0)
     rewards = jnp.sum(row_1[pl.ds(zh * NT, NT)], axis=0)
     send_row(1, jnp.sum(row_1[...], axis=0))
-    for g in range(2, kv_heads):
-        for r in range(responses):
-            attend(r, g)
+    for r, g in order[3:]:
+        attend(r, g)
     wait_rows(1)
     table = jnp.sum(row_2[...], axis=0)
     group = jnp.sum(jnp.where(lane == mine, table, 0.0), axis=1, keepdims=True) / BEST

time: 50.5 us -> 50.4 us (level)
  no operation moved by 1% of the time
where the time goes in v9:
time: 50.4 us; the launch traced here: 50.2 us
  Pallas kernels  48.2 us (96%)
  local copies, waits for them, and re-layouts  1.38 us (3%)
  between operations  0.64 us (1%)
    pallas_call x1, Pallas kernels, shards(): pl.pallas_call(kernel, out_shape=(pltpu.VMEM(response_queries.shape, bf16...  48.2 us

profile of v9, /device:TPU:1, one launch (start us, length us, event | category | flops | bytes accessed | tf_op | source)
XLA Modules:
  0.0 50.2 jit_solution(7597240043590525285)
XLA Ops:
  0.6 48.2 %shard_map.77 = (bf16[2,128,1024]{2,1,0:T(8,128)(2,1)S(1)}, f32[1,128]{1,0:T(1,128)S(1)}) custom-call(s32[2]{0:T(128)} %lengths_hbm.1, s32[128]{0:T(128)} %prompts_hbm.1, f32[8,128]{1,0:T(8,128)} %bitcast.3, bf16[2,128,1024]{2,1,0:T(8,128)(2,1)} %q_hbm.1, bf16[2,2,128,512]{3,2,1,0:T(8,128)(2,1)} %kv_hbm.1, bf16[2,16,4,512]{3,2,1,0:T(4,128)(2,1)} %raw_hbm.1), custom_call_target="tpu_custom_call" | custom-call | flops 700000000 | bytes 2000000 | tf_op jit(solution)/shard_map/pallas_call | solution.py:416
  48.9 0.8 %copy.9 = bf16[2,128,1024]{2,1,0:T(8,128)(2,1)} copy(bf16[2,128,1024]{2,1,0:T(8,128)(2,1)S(1)} %get-tuple-element.6) | data formatting | bytes 1048576
  49.7 0.6 %slice_bitcast_fusion = f32[2]{0:T(128)} fusion(f32[1,128]{1,0:T(1,128)S(1)} %get-tuple-element.5), kind=kLoop, calls=%fused_computation | loop fusion | bytes 16 | tf_op jit(solution)/shard_map/squeeze | solution.py:464

commit v10 on v7

--- a/solution.py
+++ b/solution.py
@@ -251,6 +251,8 @@
 
     for low in range(0, NXY // 2, 4):
         send_a(low, low + 4)
+    for low in range(NXY // 2, NXY - 1, 5):
+        send_a(low, low + 5)
     first[4].wait_recv()
     first[5].wait_recv()
     for copy in second[2:]:
@@ -259,8 +261,6 @@
 
     for low in range(0, NZX - 1, 5):
         send_b(low, low + 5)
-    for low in range(NXY // 2, NXY - 1, 5):
-        send_a(low, low + 5)
 
     mine = prompts[me]
     all_a[xy] = by_prompt_a[mine]

time: 50.5 us -> 50.4 us (level)
  no operation moved by 1% of the time
where the time goes in v10:
time: 50.4 us; the launch traced here: 50.3 us
  Pallas kernels  48.3 us (96%)
  local copies, waits for them, and re-layouts  1.38 us (3%)
  between operations  0.64 us (1%)
    pallas_call x1, Pallas kernels, shards(): pl.pallas_call(kernel, out_shape=(pltpu.VMEM(response_queries.shape, bf16...  48.3 us

profile of v10, /device:TPU:1, one launch (start us, length us, event | category | flops | bytes accessed | tf_op | source)
XLA Modules:
  0.0 50.3 jit_solution(2657879633995677683)
XLA Ops:
  0.6 48.3 %shard_map.77 = (bf16[2,128,1024]{2,1,0:T(8,128)(2,1)S(1)}, f32[1,128]{1,0:T(1,128)S(1)}) custom-call(s32[2]{0:T(128)} %lengths_hbm.1, s32[128]{0:T(128)} %prompts_hbm.1, f32[8,128]{1,0:T(8,128)} %bitcast.3, bf16[2,128,1024]{2,1,0:T(8,128)(2,1)} %q_hbm.1, bf16[2,2,128,512]{3,2,1,0:T(8,128)(2,1)} %kv_hbm.1, bf16[2,16,4,512]{3,2,1,0:T(4,128)(2,1)} %raw_hbm.1), custom_call_target="tpu_custom_call" | custom-call | flops 700000000 | bytes 2000000 | tf_op jit(solution)/shard_map/pallas_call | solution.py:417
  48.9 0.8 %copy.9 = bf16[2,128,1024]{2,1,0:T(8,128)(2,1)} copy(bf16[2,128,1024]{2,1,0:T(8,128)(2,1)S(1)} %get-tuple-element.6) | data formatting | bytes 1048576
  49.7 0.6 %slice_bitcast_fusion = f32[2]{0:T(128)} fusion(f32[1,128]{1,0:T(1,128)S(1)} %get-tuple-element.5), kind=kLoop, calls=%fused_computation | loop fusion | bytes 16 | tf_op jit(solution)/shard_map/squeeze | solution.py:465

commit v11 on v10

--- a/solution.py
+++ b/solution.py
@@ -145,7 +145,12 @@
             dst[p] = jnp.concatenate(parts, axis=0).astype(jnp.bfloat16)
         return c
 
-    lax.fori_loop(0, PROMPTS, split, 0)
+    def split_four(i, c):
+        for n in range(4):
+            split(4 * i + n, c)
+        return c
+
+    lax.fori_loop(0, PROMPTS // 4, split_four, 0)
 
     pl.semaphore_wait(barrier, 4 + 2 + (NX - 1) + (NT - 1))
 

time: 50.4 us -> 50.4 us (level)
  no operation moved by 1% of the time
where the time goes in v11:
time: 50.4 us; the launch traced here: 50.3 us
  Pallas kernels  48.3 us (96%)
  local copies, waits for them, and re-layouts  1.38 us (3%)
  between operations  0.64 us (1%)
    pallas_call x1, Pallas kernels, shards(): pl.pallas_call(kernel, out_shape=(pltpu.VMEM(response_queries.shape, bf16...  48.3 us

profile of v11, /device:TPU:1, one launch (start us, length us, event | category | flops | bytes accessed | tf_op | source)
XLA Modules:
  0.0 50.3 jit_solution(12760327144010154605)
XLA Ops:
  0.6 48.3 %shard_map.77 = (bf16[2,128,1024]{2,1,0:T(8,128)(2,1)S(1)}, f32[1,128]{1,0:T(1,128)S(1)}) custom-call(s32[2]{0:T(128)} %lengths_hbm.1, s32[128]{0:T(128)} %prompts_hbm.1, f32[8,128]{1,0:T(8,128)} %bitcast.3, bf16[2,128,1024]{2,1,0:T(8,128)(2,1)} %q_hbm.1, bf16[2,2,128,512]{3,2,1,0:T(8,128)(2,1)} %kv_hbm.1, bf16[2,16,4,512]{3,2,1,0:T(4,128)(2,1)} %raw_hbm.1), custom_call_target="tpu_custom_call" | custom-call | flops 700000000 | bytes 2000000 | tf_op jit(solution)/shard_map/pallas_call | solution.py:422
  48.9 0.8 %copy.9 = bf16[2,128,1024]{2,1,0:T(8,128)(2,1)} copy(bf16[2,128,1024]{2,1,0:T(8,128)(2,1)S(1)} %get-tuple-element.6) | data formatting | bytes 1048576
  49.7 0.6 %slice_bitcast_fusion = f32[2]{0:T(128)} fusion(f32[1,128]{1,0:T(1,128)S(1)} %get-tuple-element.5), kind=kLoop, calls=%fused_computation | loop fusion | bytes 16 | tf_op jit(solution)/shard_map/squeeze | solution.py:470
